TPU v7x, 128 devices: a whole 4x4x4 slice. The times are simulated.
128 devices in a mesh: dp: 8 (over x, y_hi), expert: 16 (over z, y_lo, core).
Axes of the slice: x: 4, y: 4 (y_hi: 2, y_lo: 2; y = y_hi * 2 + y_lo), z: 4, core: 2. Of those that a mesh axis runs over, the one named last changes fastest.
Arguments:
- tokens: bfloat16 [512, 256, 1280], P(('dp', 'expert')), may hold values from -64 to 64
- router: bfloat16 [1280, 128], replicated, may hold values from -2 to 2
- cotangent: bfloat16 [512, 256, 1280], P(('dp', 'expert')), may hold values from -16 to 16
- slot_out: bfloat16 [512, 128, 1280], P(('dp', 'expert')), may hold values from -6 to 6
- pre_act: bfloat16 [128, 512, 2560], P(('dp', 'expert')), may hold values from -6 to 6
- w_in: bfloat16 [128, 1280, 2560], P(('dp', 'expert')), may hold values from -0.15625 to 0.15625
- w_out: bfloat16 [128, 2560, 1280], P(('dp', 'expert')), may hold values from -0.125 to 0.125
Outputs:
- token_grad: bfloat16 [512, 256, 1280], P(('dp', 'expert'))
- router_grad: float32 [1280, 128], replicated
All inputs are finite; a program needn't handle non-finite values.
Results may differ from a plain program's by a relative error of at most 0.012.
Values may be sent and summed in bfloat16 or wider, within the bound.
No kernel may reach another device: no remote copies, remote signals or barrier semaphores. Data moves between devices by JAX's collectives and lax.ppermute only.
A program may use at most 128 MiB of HBM per device.

v0:
```python
import math

import jax
import jax.numpy as jnp
from jax import lax
from jax.sharding import PartitionSpec as P


def gelu_slope(values):
    normal_cdf = 0.5 * (1.0 + jax.scipy.special.erf(values * 2.0 ** (-0.5)))
    density = jnp.exp(-0.5 * values * values) * (2.0 * math.pi) ** (-0.5)
    return normal_cdf + values * density


def local(tokens, router, cotangent, slot_out, pre_act, w_in, w_out):
    img_dev = tokens.shape[0]
    ways_dp = lax.axis_size("dp")
    ways_exp = lax.axis_size("expert")
    logits = jnp.einsum("bmd,de->bme", tokens, router, preferred_element_type=jnp.float32)
    dispatch = jax.nn.softmax(logits, axis=1)
    combine = jax.nn.softmax(logits, axis=2)
    slot_grad = jnp.einsum(
        "bme,bmd->bed", combine.astype(jnp.bfloat16), cotangent, preferred_element_type=jnp.float32
    ).astype(jnp.bfloat16)
    arrived = lax.all_to_all(slot_grad, ("dp", "expert"), split_axis=1, concat_axis=0, tiled=True)
    combine_grad = jnp.einsum(
        "bmd,bed->bme", cotangent, slot_out, preferred_element_type=jnp.float32
    )
    from_combine = combine * (combine_grad - jnp.sum(combine * combine_grad, axis=2, keepdims=True))
    hidden_grad = jnp.einsum("red,efd->erf", arrived, w_out, preferred_element_type=jnp.float32)
    pre_grad = (hidden_grad * gelu_slope(pre_act.astype(jnp.float32))).astype(jnp.bfloat16)
    slot_back = jnp.einsum(
        "erf,edf->red", pre_grad, w_in, preferred_element_type=jnp.float32
    ).astype(jnp.bfloat16)
    returned = lax.all_to_all(slot_back, ("dp", "expert"), split_axis=0, concat_axis=1, tiled=True)
    dx_dispatch = jnp.einsum(
        "bme,bed->bmd", dispatch.astype(jnp.bfloat16), returned, preferred_element_type=jnp.float32
    )
    dispatch_grad = jnp.einsum("bmd,bed->bme", tokens, returned, preferred_element_type=jnp.float32)
    from_dispatch = dispatch * (
        dispatch_grad - jnp.sum(dispatch * dispatch_grad, axis=1, keepdims=True)
    )
    logit_grad = (from_combine + from_dispatch).astype(jnp.bfloat16)
    token_grad = (
        dx_dispatch
        + jnp.einsum("bme,de->bmd", logit_grad, router, preferred_element_type=jnp.float32)
    ).astype(jnp.bfloat16)
    router_term = jnp.einsum("bmd,bme->de", tokens, logit_grad, preferred_element_type=jnp.float32)
    router_total = lax.psum(router_term, ("dp", "expert"))
    images = img_dev * ways_dp * ways_exp
    return (token_grad, router_total / images)


def solution(mesh):
    return jax.shard_map(
        local,
        mesh=mesh,
        in_specs=(
            P(("dp", "expert"), None, None),
            P(),
            P(("dp", "expert"), None, None),
            P(("dp", "expert"), None, None),
            P(("dp", "expert"), None, None),
            P(("dp", "expert"), None, None),
            P(("dp", "expert"), None, None),
        ),
        out_specs=(P(("dp", "expert"), None, None), P()),
        check_vma=False,
    )
```

profile of v0, /device:TPU:1, one launch (start us, length us, event | category | flops | bytes accessed | tf_op | source)
XLA Modules:
  0.0 294.2 jit_solution(10943109239457836637)
XLA Ops:
  7.2 2.8 fusion.54
  9.9 1.0 fusion.65
  11.0 3.2 %convolution_convert_fusion = bf16[4,128,1280]{2,1,0:T(8,128)(2,1)} fusion(bf16[4,256,1280]{2,1,0:T(8,128)(2,1)S(1)} %copy-done, f32[4,256]{1,0:T(4,128)S(1)} %get-tuple-element.10, f32[4,256,128]{2,1,0:T(8,128)S(1)} %fusion.54), kind=kOutput, calls=%fused_computation.23 | convolution fusion | flops 336594048 | bytes 4460544 | tf_op jit(solution)/shard_map/bme,bmd->bed/dot_general | solution.py:22
  14.2 2.3 copy.33
  16.5 33.4 %all_to_all.33 = bf16[4,128,1280]{2,0,1:T(4,128)(2,1)} all-to-all(bf16[4,128,1280]{2,0,1:T(4,128)(2,1)S(1)} %copy.33), channel_id=1, replica_groups=mesh['dp'=8,'expert'=16] {'dp','expert'}, dimensions={1} | all-to-all | bytes 2621440 | tf_op jit(solution)/shard_map/all_to_all | solution.py:25
  49.9 3.4 %reshape.26 = bf16[512,1280]{1,0:T(8,128)(2,1)} reshape(bf16[128,4,1,1280]{3,1,0,2:T(4,128)(2,1)} %bitcast.70) | data formatting | bytes 2621440 | tf_op jit(solution)/shard_map/reshape
  53.3 14.0 %fusion.24 = bf16[512,1,1280]{2,0,1:T(8,128)(2,1)} fusion(bf16[1,1280,2560]{2,1,0:T(8,128)(2,1)} %param.12, bf16[1,512,2560]{2,1,0:T(8,128)(2,1)} %param.11, bf16[512,1280]{1,0:T(8,128)(2,1)} %reshape.26, bf16[1,2560,1280]{2,1,0:T(8,128)(2,1)} %param.13), kind=kOutput, calls=%fused_computation.24 | convolution fusion | flops 6725959680 | bytes 18350080 | tf_op jit(solution)/shard_map/erf,edf->red/dot_general | solution.py:32
  67.8 3.6 %reduce.1 = bf16[512,1280]{1,0:T(8,128)(2,1)} reduce(bf16[512,1,1280]{2,0,1:T(8,128)(2,1)} %fusion.24, bf16[]{:T(256)} %broadcast.8), dimensions={1}, to_apply=%copy.34.reduce_sub_computation | reduce | bytes 2621442 | tf_op jit(solution)/shard_map/convert_element_type | solution.py:34
  71.4 4.0 %reshape.33 = bf16[128,2,2560]{2,1,0:T(2,128)(2,1)} reshape(bf16[512,1280]{1,0:T(8,128)(2,1)} %reduce.1) | data formatting | bytes 2621440
  75.5 5.4 %all-to-all-start.1 = ((bf16[128,2,2560]{2,1,0:T(2,128)(2,1)}), bf16[128,2,2560]{2,1,0:T(2,128)(2,1)}, u32[]{:S(2)}, u32[]{:S(2)}) async-start(bf16[128,2,2560]{2,1,0:T(2,128)(2,1)} %reshape.33), calls=%async_computation.1 | async-start | bytes 2621440 | tf_op jit(solution)/shard_map/all_to_all | solution.py:35
  80.9 0.9 fusion.66
  81.8 3.0 %fusion.67 = f32[4,256,128]{2,1,0:T(8,128)} fusion(bf16[4,256,1280]{2,1,0:T(8,128)(2,1)S(1)} %copy-done, bf16[4,128,1280]{2,1,0:T(8,128)(2,1)} %param.10), kind=kOutput, calls=%fused_computation.65 | convolution fusion | flops 335544320 | bytes 4456448 | tf_op jit(solution)/shard_map/bmd,bed->bme/dot_general | solution.py:26
  84.8 17.9 %all-to-all-done.1 = bf16[128,2,2560]{2,1,0:T(2,128)(2,1)} async-done(((bf16[128,2,2560]{2,1,0:T(2,128)(2,1)}), bf16[128,2,2560]{2,1,0:T(2,128)(2,1)}, u32[]{:S(2)}, u32[]{:S(2)}) %all-to-all-start.1) | async-done | bytes 1310752 | tf_op jit(solution)/shard_map/all_to_all | solution.py:35
  102.7 8.9 %reshape.34 = bf16[512,1,1280]{2,1,0:T(2,128)(2,1)} reshape(bf16[128,2,2560]{2,1,0:T(2,128)(2,1)} %all-to-all-done.1) | data formatting | bytes 2621440
  111.6 10.1 %reduce = bf16[512,1280]{1,0:T(8,128)(2,1)} reduce(bf16[512,1,1280]{2,1,0:T(2,128)(2,1)} %reshape.34, bf16[]{:T(256)} %constant.25), dimensions={1}, to_apply=%all_to_all.27.reduce_sub_computation | reduce | bytes 2621442 | tf_op jit(solution)/shard_map/all_to_all | solution.py:35
  121.6 3.5 %all_to_all.28 = bf16[128,4,1,1280]{3,1,0,2:T(4,128)(2,1)} reshape(bf16[512,1280]{1,0:T(8,128)(2,1)} %reduce) | data formatting | bytes 2621440 | tf_op jit(solution)/shard_map/all_to_all | solution.py:35
  125.1 3.8 %fusion.33 = f32[4,256,128]{2,1,0:T(8,128)} fusion(bf16[4,256,1280]{2,1,0:T(8,128)(2,1)} %param.7, bf16[128,4,1,1280]{3,1,0,2:T(4,128)(2,1)} %all_to_all.28), kind=kOutput, calls=%fused_computation.32 | convolution fusion | flops 335544320 | bytes 4456448 | tf_op jit(solution)/shard_map/bmd,bed->bme/dot_general | solution.py:39
  128.9 4.5 %fusion.29 = f32[4,256,1280]{2,1,0:T(8,128)} fusion(bf16[128,4,1,1280]{3,1,0,2:T(4,128)(2,1)} %all_to_all.28, f32[4,128]{1,0:T(4,128)S(1)} %get-tuple-element.12, f32[4,256,128]{2,1,0:T(8,128)S(1)} %fusion.54), kind=kOutput, calls=%fused_computation.28 | convolution fusion | flops 335938304 | bytes 7079936 | tf_op jit(solution)/shard_map/bme,bed->bmd/dot_general | solution.py:36
  133.4 1.7 fusion.42
  135.1 8.6 %convolution_bitcast_fusion = f32[1280,128]{0,1:T(8,128)} fusion(bf16[4,256,1280]{2,1,0:T(8,128)(2,1)} %param.7, f32[4,256,128]{2,1,0:T(8,128)S(1)} %fusion.42, f32[4,256,128]{2,1,0:T(8,128)} %fusion.67, f32[4,256,128]{2,1,0:T(8,128)} %get-tuple-element.11, f32[4,256]{1,0:T(4,128)S(1)} %get-tuple-element.10), kind=kOutput, calls=%fused_computation.25 | convolution fusion | flops 336462976 | bytes 4853760 | tf_op jit(solution)/shard_map/bmd,bme->de/dot_general | solution.py:48
  143.7 9.4 %add_convert_fusion = bf16[4,256,1280]{2,1,0:T(8,128)(2,1)} fusion(f32[4,256,1280]{2,1,0:T(8,128)} %fusion.29, f32[4,256,128]{2,1,0:T(8,128)S(1)} %fusion.42, f32[4,256,128]{2,1,0:T(8,128)} %fusion.67, bf16[1280,128]{1,0:T(8,128)(2,1)S(1)} %copy-done.1, f32[4,256,128]{2,1,0:T(8,128)} %get-tuple-element.11, f32[4,256]{1,0:T(4,128)S(1)} %get-tuple-element.10), kind=kOutput, calls=%fused_computation.19 | convolution fusion | flops 339084416 | bytes 9768960 | tf_op jit(solution)/shard_map/bme,de->bmd/dot_general | solution.py:46
  153.1 132.1 %all-reduce.2.cloned.1.call-done = f32[1280,128]{0,1:T(8,128)} async-done(((f32[1280,128]{0,1:T(8,128)}), f32[1280,128]{0,1:T(8,128)}) %all-reduce.2.cloned.1.call-update) | async-done | bytes 655376 | tf_op jit(solution)/shard_map/psum | solution.py:49
  285.2 1.1 broadcast_multiply_fusion
  286.3 1.1 copy.40
  (7 shorter events, 0.6 us)
Async XLA Ops:
  7.2 3.8 %copy-start = (bf16[4,256,1280]{2,1,0:T(8,128)(2,1)S(1)}, bf16[4,256,1280]{2,1,0:T(8,128)(2,1)}, u32[]{:S(2)}) copy-start(bf16[4,256,1280]{2,1,0:T(8,128)(2,1)} %param.9) | copy-start | bytes 7864324
  75.5 27.2 %all-to-all-start.1 = ((bf16[128,2,2560]{2,1,0:T(2,128)(2,1)}), bf16[128,2,2560]{2,1,0:T(2,128)(2,1)}, u32[]{:S(2)}, u32[]{:S(2)}) async-start(bf16[128,2,2560]{2,1,0:T(2,128)(2,1)} %reshape.33), calls=%async_computation.1 | async-start | bytes 2621440 | tf_op jit(solution)/shard_map/all_to_all | solution.py:35
  80.9 204.3 %all-reduce.2.cloned.1.call-start = ((), (), s32[]{:S(2)}) async-start(), calls=%async_computation.2 | async-start | bytes 1310720 | tf_op jit(solution)/shard_map/psum | solution.py:49
  135.1 8.6 %copy-start.1 = (bf16[1280,128]{1,0:T(8,128)(2,1)S(1)}, bf16[1280,128]{1,0:T(8,128)(2,1)}, u32[]{:S(2)}) copy-start(bf16[1280,128]{1,0:T(8,128)(2,1)} %param.8) | copy-start | bytes 983044
Sparse Core Ops, SparseCore 0:
  143.8 141.3 all-reduce.1
where the time goes:
time: 295 us; the launch traced here: 294 us
  waiting for transfers between devices  150 us (51%)
  matrix products  49.3 us (17%)
  blocking collectives  33.4 us (11%)
  local copies, waits for them, and re-layouts  23.7 us (8%)
  other arithmetic  18.4 us (6%)
  between operations  14.1 us (5%)
  starting transfers between devices  5.45 us (2%)
    psum x1, waiting for transfers between devices, local(): router_total = lax.psum(router_term, ('dp', 'expert'))  132 us
    all_to_all x1, blocking collectives, local(): lax.all_to_all(slot_grad, ('dp', 'expert'), split_axis=1, concat_axis=0,...  33.4 us
    all_to_all x1, waiting for transfers between devices, local(): lax.all_to_all(slot_back, ('dp', 'expert'), split_axis=0, concat_axis=1,...  17.9 us
    dot_general x1, matrix products, local(): jnp.einsum('erf,edf->red', pre_grad, w_in, preferred_element_type=jnp.flo...  14 us
    unnamed x7, local copies, waits for them, and re-layouts  14 us
    all_to_all x1, other arithmetic, local(): lax.all_to_all(slot_back, ('dp', 'expert'), split_axis=0, concat_axis=1,...  10.1 us
    dot_general x1, matrix products, local(): jnp.einsum('bme,de->bmd', logit_grad, router, preferred_element_type=jnp....  9.41 us
    dot_general x1, matrix products, local(): jnp.einsum('bmd,bme->de', tokens, logit_grad, preferred_element_type=jnp....  8.6 us
  transfers between devices with their start and end apart: 2, of which 2 were waited for; matrix products, arithmetic and copies ran while one was open for 5% of the time, Pallas kernels for 0%

commit v1 on v0

v1 whole, which is shorter than its diff:
```python
import functools
import math

import jax
import jax.numpy as jnp
from jax import lax
from jax.experimental import pallas as pl
from jax.experimental.pallas import tpu as pltpu
from jax.sharding import PartitionSpec as P

AXES = ("dp", "expert")
BF = jnp.bfloat16
F32 = jnp.float32
LANES = 128
MIB = 1 << 20


def cost(flops, nbytes, trans=0):
    return pl.CostEstimate(flops=flops, bytes_accessed=nbytes, transcendentals=trans)


def gelu_slope(values):
    normal_cdf = 0.5 * (1.0 + jax.scipy.special.erf(values * 2.0 ** (-0.5)))
    density = jnp.exp(-0.5 * values * values) * (2.0 * math.pi) ** (-0.5)
    return normal_cdf + values * density


def dot(a, b, ca, cb):
    return lax.dot_general(a, b, (((ca,), (cb,)), ((), ())), preferred_element_type=F32)


def softmax(logits, axis):
    e = jnp.exp(logits - jnp.max(logits, axis=axis, keepdims=True))
    return e / jnp.sum(e, axis=axis, keepdims=True)


def front_kernel(tok_ref, router_ref, cot_ref, sg_ref, logits_ref, rows):
    b = pl.program_id(0)
    n = pl.num_programs(0)
    logits = dot(tok_ref[0], router_ref[...], 1, 0)
    logits_ref[0] = logits
    combine = softmax(logits, 1).astype(BF)
    slot_grad = dot(combine, cot_ref[0], 0, 0)
    half_tiles = rows.shape[0]
    experts = slot_grad.shape[0]
    stride = rows.shape[1] // experts
    for t in range(2 * half_tiles):
        h, j = divmod(t, half_tiles)
        rows[j, pl.ds(2 * b + h, experts, stride), :] = slot_grad[:, t * LANES : (t + 1) * LANES]

    @pl.when(b == n - 1)
    def _():
        for j in range(half_tiles):
            sg_ref[:, j * LANES : (j + 1) * LANES] = rows[j].astype(BF)


def front(tokens, router, cotangent):
    images, m, d = tokens.shape
    experts = router.shape[1]
    total = experts * images * 2
    return pl.pallas_call(
        front_kernel,
        grid=(images,),
        in_specs=[
            pl.BlockSpec((1, m, d), lambda b: (b, 0, 0)),
            pl.BlockSpec((d, experts), lambda b: (0, 0)),
            pl.BlockSpec((1, m, d), lambda b: (b, 0, 0)),
        ],
        out_specs=[
            pl.BlockSpec((total, d // 2), lambda b: (0, 0)),
            pl.BlockSpec((1, m, experts), lambda b: (b, 0, 0)),
        ],
        out_shape=[
            jax.ShapeDtypeStruct((total, d // 2), BF),
            jax.ShapeDtypeStruct((images, m, experts), F32),
        ],
        scratch_shapes=[pltpu.VMEM((d // 2 // LANES, total, LANES), F32)],
        compiler_params=pltpu.CompilerParams(vmem_limit_bytes=24 * MIB),
        cost_estimate=cost(4 * images * m * d * experts, 4 * images * m * d + 4 * total * d),
        name="front",
    )(tokens, router, cotangent)


def expert_kernel(x_ref, wo_ref, wi_ref, slope_ref, out_ref, wide, r_ref, pg_ref):
    half_tiles, total, _ = wide.shape
    count = total // 2
    for j in range(half_tiles):
        wide[j] = x_ref[:, j * LANES : (j + 1) * LANES].astype(F32)
    for t in range(2 * half_tiles):
        h, j = divmod(t, half_tiles)
        r_ref[:, t * LANES : (t + 1) * LANES] = wide[j, pl.ds(h, count, 2), :].astype(BF)
    step = 256

    @pl.loop(0, wo_ref.shape[0] // step)
    def _(c):
        cols = pl.ds(pl.multiple_of(c * step, step), step)
        hidden = dot(r_ref[...], wo_ref[cols, :], 1, 1)
        pg_ref[:, cols] = (hidden * slope_ref[:, cols]).astype(BF)

    for c in range(wi_ref.shape[0] // step):
        back = dot(pg_ref[...], wi_ref[c * step : (c + 1) * step, :], 1, 1)
        for u in range(step // LANES):
            h, j = divmod(c * (step // LANES) + u, half_tiles)
            wide[j, pl.ds(h, count, 2), :] = back[:, u * LANES : (u + 1) * LANES]
    for j in range(half_tiles):
        out_ref[:, j * LANES : (j + 1) * LANES] = wide[j].astype(BF)


def expert(x, w_out, w_in, slope):
    total, half = x.shape
    ff, d = w_out.shape
    vmem = pl.BlockSpec(memory_space=pltpu.VMEM)
    return pl.pallas_call(
        expert_kernel,
        in_specs=[vmem] * 4,
        out_specs=vmem,
        out_shape=jax.ShapeDtypeStruct((total, half), BF),
        scratch_shapes=[
            pltpu.VMEM((half // LANES, total, LANES), F32),
            pltpu.VMEM((total // 2, d), BF),
            pltpu.VMEM((total // 2, ff), BF),
        ],
        compiler_params=pltpu.CompilerParams(vmem_limit_bytes=48 * MIB),
        cost_estimate=cost(2 * total * d * ff, 4 * ff * d + 2 * total * ff),
        name="expert",
    )(x, w_out, w_in, slope)


def back(y, tokens, dispatch, from_combine):
    images, m, d = tokens.shape
    experts = dispatch.shape[2]
    total, half = y.shape
    wide_cols = 2 * LANES
    return pl.pallas_call(
        functools.partial(back_kernel, -(-d // LANES // (total // experts))),
        grid=(images,),
        in_specs=[
            pl.BlockSpec((total, half), lambda b: (0, 0)),
            pl.BlockSpec((1, m, d), lambda b: (b, 0, 0)),
            pl.BlockSpec((1, m, experts), lambda b: (b, 0, 0)),
            pl.BlockSpec((1, m, experts), lambda b: (b, 0, 0)),
        ],
        out_specs=[
            pl.BlockSpec((1, m, experts), lambda b: (b, 0, 0)),
            pl.BlockSpec((1, experts, d), lambda b: (b, 0, 0)),
            pl.BlockSpec((total, wide_cols), lambda b: (0, 0)),
        ],
        out_shape=[
            jax.ShapeDtypeStruct((images, m, experts), BF),
            jax.ShapeDtypeStruct((images, experts, d), BF),
            jax.ShapeDtypeStruct((total, wide_cols), BF),
        ],
        scratch_shapes=[
            pltpu.VMEM((half // LANES, total, LANES), F32),
            pltpu.VMEM((experts, d), F32),
        ],
        compiler_params=pltpu.CompilerParams(vmem_limit_bytes=24 * MIB),
        cost_estimate=cost(4 * images * m * d * experts, 4 * images * m * d),
        name="back",
    )(y, tokens, dispatch, from_combine)


def back_kernel(groups, y_ref, tok_ref, disp_ref, fc_ref, lg_ref, sb_ref, term_ref, wide, acc):
    b = pl.program_id(0)
    n = pl.num_programs(0)
    half_tiles, total, _ = wide.shape
    experts = sb_ref.shape[1]
    stride = total // experts

    @pl.when(b == 0)
    def _():
        acc[...] = jnp.zeros_like(acc)
        for j in range(half_tiles):
            wide[j] = y_ref[:, j * LANES : (j + 1) * LANES].astype(F32)

    for t in range(2 * half_tiles):
        h, j = divmod(t, half_tiles)
        sb_ref[0, :, t * LANES : (t + 1) * LANES] = wide[j, pl.ds(2 * b + h, experts, stride), :].astype(BF)
    tok = tok_ref[0]
    disp = disp_ref[0]
    grad = dot(tok, sb_ref[0], 1, 1)
    from_dispatch = disp * (grad - jnp.sum(disp * grad, axis=0, keepdims=True))
    logit_grad = fc_ref[0] + from_dispatch
    lg_ref[0] = logit_grad.astype(BF)
    acc[...] += dot(logit_grad.T.astype(BF), tok, 1, 0)

    @pl.when(b == n - 1)
    def _():
        tiles = acc.shape[1] // LANES
        for t in range(groups * stride):
            part = acc[:, t * LANES : (t + 1) * LANES] if t < tiles else jnp.zeros((experts, LANES), F32)
            j, r = divmod(t, stride)
            wide[j, pl.ds(r, experts, stride), :] = part
        for j in range(groups):
            term_ref[:, j * LANES : (j + 1) * LANES] = wide[j].astype(BF)


def token_kernel(disp_ref, lg_ref, sb_ref, router_t_ref, out_ref):
    left = jnp.concatenate([disp_ref[0].astype(BF), lg_ref[0]], axis=1)
    right = jnp.concatenate([sb_ref[0], router_t_ref[...]], axis=0)
    out_ref[0] = dot(left, right, 1, 0).astype(BF)


def token_side(dispatch, logit_grad, slot_back, router_t):
    images, m, experts = dispatch.shape
    d = router_t.shape[1]
    return pl.pallas_call(
        token_kernel,
        grid=(images,),
        in_specs=[
            pl.BlockSpec((1, m, experts), lambda b: (b, 0, 0)),
            pl.BlockSpec((1, m, experts), lambda b: (b, 0, 0)),
            pl.BlockSpec((1, experts, d), lambda b: (b, 0, 0)),
            pl.BlockSpec((experts, d), lambda b: (0, 0)),
        ],
        out_specs=pl.BlockSpec((1, m, d), lambda b: (b, 0, 0)),
        out_shape=jax.ShapeDtypeStruct((images, m, d), BF),
        compiler_params=pltpu.CompilerParams(vmem_limit_bytes=24 * MIB),
        cost_estimate=cost(4 * images * m * d * experts, 4 * images * m * d),
        name="token_side",
    )(dispatch, logit_grad, slot_back, router_t)


def sum_kernel(scale, x_ref, out_ref):
    devices = out_ref.shape[0]
    total = jnp.sum(x_ref[...].astype(F32), axis=0, keepdims=True) * scale
    out_ref[...] = jnp.broadcast_to(total, out_ref.shape).astype(BF)


def sum_terms(x, scale):
    return pl.pallas_call(
        functools.partial(sum_kernel, scale),
        in_specs=[pl.BlockSpec(memory_space=pltpu.VMEM)],
        out_specs=pl.BlockSpec(memory_space=pltpu.VMEM),
        out_shape=jax.ShapeDtypeStruct(x.shape, BF),
        compiler_params=pltpu.CompilerParams(vmem_limit_bytes=24 * MIB),
        cost_estimate=cost(x.size, 4 * x.size),
        name="sum_terms",
    )(x)


def finish_kernel(x_ref, out_ref, wide):
    groups, total, _ = wide.shape
    experts = out_ref.shape[1]
    stride = total // experts
    for j in range(groups):
        wide[j] = x_ref[:, j * LANES : (j + 1) * LANES].astype(F32)
    for t in range(out_ref.shape[0] // LANES):
        j, r = divmod(t, stride)
        out_ref[t * LANES : (t + 1) * LANES, :] = wide[j, pl.ds(r, experts, stride), :].T


def finish(x, d, experts):
    total, cols = x.shape
    return pl.pallas_call(
        finish_kernel,
        in_specs=[pl.BlockSpec(memory_space=pltpu.VMEM)],
        out_specs=pl.BlockSpec(memory_space=pltpu.VMEM),
        out_shape=jax.ShapeDtypeStruct((d, experts), F32),
        scratch_shapes=[pltpu.VMEM((cols // LANES, total, LANES), F32)],
        compiler_params=pltpu.CompilerParams(vmem_limit_bytes=24 * MIB),
        cost_estimate=cost(x.size, 6 * x.size),
        name="finish",
    )(x)


def exchange(x, devices):
    rows, cols = x.shape
    x = x.reshape(devices, rows // devices, cols)
    return lax.all_to_all(x, AXES, split_axis=0, concat_axis=0, tiled=True).reshape(rows, cols)


def local(tokens, router, cotangent, slot_out, pre_act, w_in, w_out):
    img_dev, m, d = tokens.shape
    experts = router.shape[1]
    devices = lax.axis_size("dp") * lax.axis_size("expert")
    slot_grad, logits = front(tokens, router, cotangent)
    arrived = exchange(slot_grad, devices)

    slope = gelu_slope(pre_act[0].astype(F32))
    combine = jax.nn.softmax(logits, axis=2)
    dispatch = jax.nn.softmax(logits, axis=1)
    combine_grad = jnp.einsum("bmd,bed->bme", cotangent, slot_out, preferred_element_type=F32)
    from_combine = combine * (combine_grad - jnp.sum(combine * combine_grad, axis=2, keepdims=True))

    slot_back = expert(arrived, w_out[0], w_in[0], slope)
    returned = exchange(slot_back, devices)
    logit_grad, slot_back, term = back(returned, tokens, dispatch, from_combine)
    terms = exchange(term, devices)
    token_grad = token_side(dispatch, logit_grad, slot_back, router.T)
    stride = img_dev * 2
    total = sum_terms(terms.reshape(devices, stride, -1), 1.0 / (img_dev * devices))
    gathered = exchange(total.reshape(devices * stride, -1), devices)
    return token_grad, finish(gathered, d, experts)


def solution(mesh):
    spec = P(AXES, None, None)
    return jax.shard_map(
        local,
        mesh=mesh,
        in_specs=(spec, P(), spec, spec, spec, spec, spec),
        out_specs=(spec, P()),
        check_vma=False,
    )
```

time: 295 us -> 134 us (0.45)
  waiting for transfers between devices: 150 us -> 39.4 us
  matrix products: 49.3 us -> 5.22 us
  Pallas kernels: 0 us -> 28 us
  blocking collectives: 33.4 us -> 17.8 us
  starting transfers between devices: 5.45 us -> 19.5 us
  between operations: 14.1 us -> 0.76 us
  local copies, waits for them, and re-layouts: 23.7 us -> 12.8 us
  other arithmetic: 18.4 us -> 9.35 us
    psum x1 -> x0, waiting for transfers between devices: 132 us -> none  [local(): router_total = lax.psum(router_term, ('dp', 'expert'))]
    dot_general x8 -> x0, matrix products: 49.3 us -> none  [the longest x1 14 us: local(): jnp.einsum('erf,edf->red', pre_grad, w_in, preferred_element_type=jnp.flo...]
    pallas_call x0 -> x6, Pallas kernels: none -> 28 us  [the longest x1 15.8 us: expert(): pl.pallas_call(expert_kernel, in_specs=[vmem] * 4, out_specs=vmem, out_sh...]
    all_to_all x1 -> x3, waiting for transfers between devices: 17.9 us -> 39.4 us  [exchange(): lax.all_to_all(x, AXES, split_axis=0, concat_axis=0, tiled=True)]
    all_to_all x1, blocking collectives: 33.4 us -> 17.8 us  [exchange(): lax.all_to_all(x, AXES, split_axis=0, concat_axis=0, tiled=True)]
    all_to_all x1 -> x3, starting transfers between devices: 5.41 us -> 19.5 us  [exchange(): lax.all_to_all(x, AXES, split_axis=0, concat_axis=0, tiled=True)]
    all_to_all x1 -> x0, other arithmetic: 10.1 us -> none  [local(): lax.all_to_all(slot_back, ('dp', 'expert'), split_axis=0, concat_axis=1,...]
    add x0 -> x1, other arithmetic: none -> 5.53 us  [gelu_slope(): return normal_cdf + values * density]
  transfers between devices with their start and end apart: 2 -> 3, of which waited for: 2 -> 3; matrix products, arithmetic and copies ran while one was open for 5% -> 11% of each run, Pallas kernels for 0% -> 2%
where the time goes in v1:
time: 134 us; the launch traced here: 133 us
  waiting for transfers between devices  39.4 us (29%)
  Pallas kernels  28 us (21%)
  starting transfers between devices  19.5 us (15%)
  blocking collectives  17.8 us (13%)
  local copies, waits for them, and re-layouts  12.8 us (10%)
  other arithmetic  9.35 us (7%)
  matrix products  5.22 us (4%)
    all_to_all x3, waiting for transfers between devices, exchange(): lax.all_to_all(x, AXES, split_axis=0, concat_axis=0, tiled=True)  39.4 us
    all_to_all x3, starting transfers between devices, exchange(): lax.all_to_all(x, AXES, split_axis=0, concat_axis=0, tiled=True)  19.5 us
    all_to_all x1, blocking collectives, exchange(): lax.all_to_all(x, AXES, split_axis=0, concat_axis=0, tiled=True)  17.8 us
    pallas_call x1, Pallas kernels, expert(): pl.pallas_call(expert_kernel, in_specs=[vmem] * 4, out_specs=vmem, out_sh...  15.8 us
    unnamed x25, local copies, waits for them, and re-layouts  12.8 us
    add x1, other arithmetic, gelu_slope(): return normal_cdf + values * density  5.53 us
    sub x1, matrix products, local(): combine_grad - jnp.sum(combine * combine_grad, axis=2, keepdims=True)  5.22 us
    pallas_call x1, Pallas kernels, back(): pl.pallas_call(functools.partial(back_kernel, -(-d // LANES // (total //...  4 us
  transfers between devices with their start and end apart: 3, of which 3 were waited for; matrix products, arithmetic and copies ran while one was open for 11% of the time, Pallas kernels for 2%

profile of v1, /device:TPU:1, one launch (start us, length us, event | category | flops | bytes accessed | tf_op | source)
XLA Modules:
  0.0 132.9 jit_solution(5461594136825259657)
XLA Ops:
  0.7 1.8 %copy-done.1 = bf16[4,256,1280]{2,1,0:T(8,128)(2,1)S(1)} copy-done((bf16[4,256,1280]{2,1,0:T(8,128)(2,1)S(1)}, bf16[4,256,1280]{2,1,0:T(8,128)(2,1)}, u32[]{:S(2)}) %copy-start.1) | copy-done | bytes 2621464
  2.5 1.7 %copy-done.3 = bf16[4,256,1280]{2,1,0:T(8,128)(2,1)S(1)} copy-done((bf16[4,256,1280]{2,1,0:T(8,128)(2,1)S(1)}, bf16[4,256,1280]{2,1,0:T(8,128)(2,1)}, u32[]{:S(2)}) %copy-start.3) | copy-done | bytes 2621464
  5.2 3.4 %front.1 = (bf16[1024,640]{1,0:T(8,128)(2,1)S(1)}, f32[4,256,128]{2,1,0:T(8,128)S(1)}) custom-call(bf16[4,256,1280]{2,1,0:T(8,128)(2,1)S(1)} %copy-done.1, bf16[1280,128]{1,0:T(8,128)(2,1)S(1)} %copy-done.8, bf16[4,256,1280]{2,1,0:T(8,128)(2,1)S(1)} %copy-done.3), custom_call_target="tpu_custom_call" | custom-call | flops 671088640 | bytes 10485760 | tf_op jit(solution)/shard_map/front/pallas_call | solution.py:61
  8.6 1.0 copy-done.5
  10.5 11.5 %all-to-all-start = ((bf16[128,8,640]{2,1,0:T(8,128)(2,1)}), bf16[128,8,640]{2,1,0:T(8,128)(2,1)S(1)}, u32[]{:S(2)}, u32[]{:S(2)}) async-start(bf16[128,8,640]{2,1,0:T(8,128)(2,1)} %bitcast.23), calls=%async_computation | async-start | bytes 2621440 | tf_op jit(solution)/shard_map/all_to_all | solution.py:270
  22.0 5.5 %fusion.8.slope_ref = f32[512,2560]{1,0:T(8,128)} fusion(bf16[1,512,2560]{2,1,0:T(8,128)(2,1)} %param.11), kind=kLoop, calls=%fused_computation.12 | loop fusion | flops 11796480 | bytes 7864320 | tf_op jit(solution)/shard_map/add | solution.py:25
  27.5 16.4 %all-to-all-done = bf16[128,8,640]{2,1,0:T(8,128)(2,1)S(1)} async-done(((bf16[128,8,640]{2,1,0:T(8,128)(2,1)}), bf16[128,8,640]{2,1,0:T(8,128)(2,1)S(1)}, u32[]{:S(2)}, u32[]{:S(2)}) %all-to-all-start) | async-done | bytes 1310752 | tf_op jit(solution)/shard_map/all_to_all | solution.py:270
  43.9 15.8 %expert.1 = bf16[1024,640]{1,0:T(8,128)(2,1)S(1)} custom-call(bf16[1024,640]{1,0:T(8,128)(2,1)S(1)} %bitcast.22, bf16[2560,1280]{1,0:T(8,128)(2,1)} %bitcast.25, bf16[1280,2560]{1,0:T(8,128)(2,1)} %bitcast.26, f32[512,2560]{1,0:T(8,128)} %fusion.8.slope_ref), custom_call_target="tpu_custom_call" | custom-call | flops 6710886400 | bytes 18350080 | tf_op jit(solution)/shard_map/expert/pallas_call | solution.py:113
  59.8 1.0 copy-done.4
  60.8 4.2 %all-to-all-start.1 = ((bf16[128,8,640]{2,1,0:T(8,128)(2,1)}), bf16[128,8,640]{2,1,0:T(8,128)(2,1)S(1)}, u32[]{:S(2)}, u32[]{:S(2)}) async-start(bf16[128,8,640]{2,1,0:T(8,128)(2,1)} %bitcast.21), calls=%async_computation.1 | async-start | bytes 2621440 | tf_op jit(solution)/shard_map/all_to_all | solution.py:270
  65.1 1.4 %fusion.12.disp_ref = f32[4,256,128]{2,1,0:T(8,128)S(1)} fusion(f32[4,256,128]{2,1,0:T(8,128)} %copy-done.11), kind=kOutput, calls=%fused_computation.16 | output fusion | flops 263678 | bytes 1048576 | tf_op jit(solution)/shard_map/div | solution.py:282
  66.5 2.4 %fusion.14 = f32[4,256,128]{2,1,0:T(8,128)} fusion(f32[4,256,128]{2,1,0:T(8,128)} %copy-done.11), kind=kOutput, calls=%fused_computation.18 | output fusion | flops 264446 | bytes 1048576 | tf_op jit(solution)/shard_map/div | solution.py:281
  68.9 5.2 %fusion.18.fc_ref = f32[4,256,128]{2,1,0:T(8,128)} fusion(f32[4,256,128]{2,1,0:T(8,128)} %fusion.14, bf16[4,256,1280]{2,1,0:T(8,128)(2,1)} %cot_ref.1, bf16[4,128,1280]{2,1,0:T(8,128)(2,1)S(1)} %copy-done), kind=kOutput, calls=%fused_computation.22 | convolution fusion | flops 671483008 | bytes 4980736 | tf_op jit(solution)/shard_map/sub | solution.py:284
  74.1 13.1 %all-to-all-done.1 = bf16[128,8,640]{2,1,0:T(8,128)(2,1)S(1)} async-done(((bf16[128,8,640]{2,1,0:T(8,128)(2,1)}), bf16[128,8,640]{2,1,0:T(8,128)(2,1)S(1)}, u32[]{:S(2)}, u32[]{:S(2)}) %all-to-all-start.1) | async-done | bytes 1310752 | tf_op jit(solution)/shard_map/all_to_all | solution.py:270
  87.2 1.7 %copy-done.2 = bf16[4,256,1280]{2,1,0:T(8,128)(2,1)S(1)} copy-done((bf16[4,256,1280]{2,1,0:T(8,128)(2,1)S(1)}, bf16[4,256,1280]{2,1,0:T(8,128)(2,1)}, u32[]{:S(2)}) %copy-start.2) | copy-done | bytes 2621464
  88.9 1.0 copy-done.10
  90.0 4.0 %back.1 = (bf16[4,256,128]{2,1,0:T(8,128)(2,1)S(1)}, bf16[4,128,1280]{2,1,0:T(8,128)(2,1)S(1)}, bf16[1024,256]{1,0:T(8,128)(2,1)S(1)}) custom-call(bf16[1024,640]{1,0:T(8,128)(2,1)S(1)} %bitcast.18, bf16[4,256,1280]{2,1,0:T(8,128)(2,1)S(1)} %copy-done.2, f32[4,256,128]{2,1,0:T(8,128)S(1)} %fusion.12.disp_ref, f32[4,256,128]{2,1,0:T(8,128)S(1)} %copy-done.10), custom_call_target="tpu_custom_call" | custom-call | flops 671088640 | bytes 5242880 | tf_op jit(solution)/shard_map/back/pallas_call | solution.py:134
  94.0 1.0 copy-done.6
  95.0 17.8 %all_to_all.20.x_ref = bf16[128,8,256]{2,1,0:T(8,128)(2,1)S(1)} all-to-all(bf16[128,8,256]{2,1,0:T(8,128)(2,1)S(1)} %bitcast.24), channel_id=1, replica_groups=mesh['dp'=8,'expert'=16] {'dp','expert'}, dimensions={0} | all-to-all | bytes 1048576 | tf_op jit(solution)/shard_map/all_to_all | solution.py:270
  113.8 3.8 %all-to-all-start.3 = ((bf16[128,8,256]{2,1,0:T(8,128)(2,1)}), bf16[128,8,256]{2,1,0:T(8,128)(2,1)S(1)}, u32[]{:S(2)}, u32[]{:S(2)}) async-start(bf16[128,8,256]{2,1,0:T(8,128)(2,1)} %sum_terms.1), calls=%async_computation.3 | async-start | bytes 1048576 | tf_op jit(solution)/shard_map/all_to_all | solution.py:270
  117.9 1.3 copy-done.7
  119.2 2.7 %token_side.1 = bf16[4,256,1280]{2,1,0:T(8,128)(2,1)} custom-call(f32[4,256,128]{2,1,0:T(8,128)S(1)} %fusion.12.disp_ref, bf16[4,256,128]{2,1,0:T(8,128)(2,1)S(1)} %get-tuple-element.9.lg_ref, bf16[4,128,1280]{2,1,0:T(8,128)(2,1)S(1)} %copy-done.7, bf16[128,1280]{1,0:T(8,128)(2,1)S(1)} %bitcast.20), custom_call_target="tpu_custom_call" | custom-call | flops 671088640 | bytes 5242880 | tf_op jit(solution)/shard_map/token_side/pallas_call | solution.py:207
  121.9 9.9 %all-to-all-done.3 = bf16[128,8,256]{2,1,0:T(8,128)(2,1)S(1)} async-done(((bf16[128,8,256]{2,1,0:T(8,128)(2,1)}), bf16[128,8,256]{2,1,0:T(8,128)(2,1)S(1)}, u32[]{:S(2)}, u32[]{:S(2)}) %all-to-all-start.3) | async-done | bytes 524320 | tf_op jit(solution)/shard_map/all_to_all | solution.py:270
  131.8 1.1 finish.1
  (18 shorter events, 2.9 us)
Async XLA Ops:
  0.6 68.3 %copy-start = (bf16[4,128,1280]{2,1,0:T(8,128)(2,1)S(1)}, bf16[4,128,1280]{2,1,0:T(8,128)(2,1)}, u32[]{:S(2)}) copy-start(bf16[4,128,1280]{2,1,0:T(8,128)(2,1)} %param.10) | copy-start | bytes 3932164
  0.6 1.8 %copy-start.1 = (bf16[4,256,1280]{2,1,0:T(8,128)(2,1)S(1)}, bf16[4,256,1280]{2,1,0:T(8,128)(2,1)}, u32[]{:S(2)}) copy-start(bf16[4,256,1280]{2,1,0:T(8,128)(2,1)} %tok_ref.3) | copy-start | bytes 7864324
  2.5 1.7 %copy-start.3 = (bf16[4,256,1280]{2,1,0:T(8,128)(2,1)S(1)}, bf16[4,256,1280]{2,1,0:T(8,128)(2,1)}, u32[]{:S(2)}) copy-start(bf16[4,256,1280]{2,1,0:T(8,128)(2,1)} %cot_ref.1) | copy-start | bytes 7864324
  4.2 1.0 copy-start.8
  8.6 1.1 copy-start.5
  9.7 0.8 copy-start.11
  10.5 33.5 %all-to-all-start = ((bf16[128,8,640]{2,1,0:T(8,128)(2,1)}), bf16[128,8,640]{2,1,0:T(8,128)(2,1)S(1)}, u32[]{:S(2)}, u32[]{:S(2)}) async-start(bf16[128,8,640]{2,1,0:T(8,128)(2,1)} %bitcast.23), calls=%async_computation | async-start | bytes 2621440 | tf_op jit(solution)/shard_map/all_to_all | solution.py:270
  59.8 1.1 copy-start.4
  60.8 26.3 %all-to-all-start.1 = ((bf16[128,8,640]{2,1,0:T(8,128)(2,1)}), bf16[128,8,640]{2,1,0:T(8,128)(2,1)S(1)}, u32[]{:S(2)}, u32[]{:S(2)}) async-start(bf16[128,8,640]{2,1,0:T(8,128)(2,1)} %bitcast.21), calls=%async_computation.1 | async-start | bytes 2621440 | tf_op jit(solution)/shard_map/all_to_all | solution.py:270
  87.2 1.7 %copy-start.2 = (bf16[4,256,1280]{2,1,0:T(8,128)(2,1)S(1)}, bf16[4,256,1280]{2,1,0:T(8,128)(2,1)}, u32[]{:S(2)}) copy-start(bf16[4,256,1280]{2,1,0:T(8,128)(2,1)} %tok_ref.3) | copy-start | bytes 7864324
  88.9 1.0 copy-start.10
  94.0 1.1 copy-start.6
  95.0 22.6 %copy-start.9 = (bf16[1280,128]{1,0:T(8,128)(2,1)S(1)}, bf16[1280,128]{1,0:T(8,128)(2,1)}, u32[]{:S(2)}) copy-start(bf16[1280,128]{1,0:T(8,128)(2,1)} %router_ref.1) | copy-start | bytes 983044
  113.8 18.0 %all-to-all-start.3 = ((bf16[128,8,256]{2,1,0:T(8,128)(2,1)}), bf16[128,8,256]{2,1,0:T(8,128)(2,1)S(1)}, u32[]{:S(2)}, u32[]{:S(2)}) async-start(bf16[128,8,256]{2,1,0:T(8,128)(2,1)} %sum_terms.1), calls=%async_computation.3 | async-start | bytes 1048576 | tf_op jit(solution)/shard_map/all_to_all | solution.py:270
  117.9 1.3 copy-start.7

commit v2 on v1

v2 whole, which is shorter than its diff:
```python
import functools
import math

import jax
import jax.numpy as jnp
from jax import lax
from jax.experimental import pallas as pl
from jax.experimental.pallas import tpu as pltpu
from jax.sharding import PartitionSpec as P

AXES = ("dp", "expert")
BF = jnp.bfloat16
F32 = jnp.float32
LANES = 128
MIB = 1 << 20


def cost(flops, nbytes, trans=0):
    return pl.CostEstimate(flops=flops, bytes_accessed=nbytes, transcendentals=trans)


def hbm(x):
    return pltpu.with_memory_space_constraint(x, pltpu.HBM)


def vmem(x):
    return pltpu.with_memory_space_constraint(x, pltpu.VMEM)


WHOLE = pl.BlockSpec(memory_space=pltpu.VMEM)


def gelu_slope(values):
    normal_cdf = 0.5 * (1.0 + jax.scipy.special.erf(values * 2.0 ** (-0.5)))
    density = jnp.exp(-0.5 * values * values) * (2.0 * math.pi) ** (-0.5)
    return normal_cdf + values * density


def dot(a, b, ca, cb):
    return lax.dot_general(a, b, (((ca,), (cb,)), ((), ())), preferred_element_type=F32)


def softmax(logits, axis):
    e = jnp.exp(logits - jnp.max(logits, axis=axis, keepdims=True))
    return e / jnp.sum(e, axis=axis, keepdims=True)


def front_kernel(tok_ref, router_ref, cot_ref, sg_ref, logits_ref, rows):
    b = pl.program_id(0)
    n = pl.num_programs(0)
    logits = dot(tok_ref[0], router_ref[...], 1, 0)
    logits_ref[0] = logits
    combine = softmax(logits, 1).astype(BF)
    slot_grad = dot(combine, cot_ref[0], 0, 0)
    half_tiles = rows.shape[0]
    experts = slot_grad.shape[0]
    stride = rows.shape[1] // experts
    for t in range(2 * half_tiles):
        h, j = divmod(t, half_tiles)
        rows[j, pl.ds(2 * b + h, experts, stride), :] = slot_grad[:, t * LANES : (t + 1) * LANES]

    @pl.when(b == n - 1)
    def _():
        for j in range(half_tiles):
            sg_ref[:, j * LANES : (j + 1) * LANES] = rows[j].astype(BF)


def front(tokens, router, cotangent):
    images, m, d = tokens.shape
    experts = router.shape[1]
    total = experts * images * 2
    return pl.pallas_call(
        front_kernel,
        grid=(images,),
        in_specs=[
            pl.BlockSpec((1, m, d), lambda b: (b, 0, 0)),
            pl.BlockSpec((d, experts), lambda b: (0, 0)),
            pl.BlockSpec((1, m, d), lambda b: (b, 0, 0)),
        ],
        out_specs=[
            pl.BlockSpec((total, d // 2), lambda b: (0, 0)),
            pl.BlockSpec((1, m, experts), lambda b: (b, 0, 0)),
        ],
        out_shape=[
            pltpu.HBM((total, d // 2), BF),
            pltpu.HBM((images, m, experts), F32),
        ],
        scratch_shapes=[pltpu.VMEM((d // 2 // LANES, total, LANES), F32)],
        compiler_params=pltpu.CompilerParams(vmem_limit_bytes=24 * MIB),
        cost_estimate=cost(4 * images * m * d * experts, 4 * images * m * d + 4 * total * d),
        name="front",
    )(hbm(tokens), hbm(router), hbm(cotangent))


STEP_UP = 512
STEP_BACK = 640
WINDOW = 3


def expert_kernel(x_ref, wo_hbm, wi_hbm, slope_hbm, out_hbm, wo, wi, slope, out, wide, rows_ref, pg_ref, w_sems, slope_sems, out_sems):
    half_tiles, total, _ = wide.shape
    count = total // 2
    ff, d = wo.shape
    pieces = [(wo_hbm, wo, pl.ds(c, STEP_UP)) for c in range(0, ff, STEP_UP)]
    ups = len(pieces)
    pieces += [(wi_hbm, wi, pl.ds(c, STEP_BACK)) for c in range(0, d, STEP_BACK)]
    groups = [
        [pltpu.make_async_copy(src.at[r], dst.at[r], w_sems.at[i])] for i, (src, dst, r) in enumerate(pieces)
    ]
    for i in range(ups):
        cols = pl.ds(i * STEP_UP, STEP_UP)
        groups[i].append(pltpu.make_async_copy(slope_hbm.at[:, cols], slope.at[:, cols], slope_sems.at[i]))

    def start(i):
        for copy in groups[i]:
            copy.start()

    def arrive(i):
        for copy in groups[i]:
            copy.wait()
        if i + WINDOW < len(groups):
            start(i + WINDOW)

    for i in range(WINDOW):
        start(i)
    for j in range(half_tiles):
        wide[j] = x_ref[:, j * LANES : (j + 1) * LANES].astype(F32)
    for t in range(2 * half_tiles):
        h, j = divmod(t, half_tiles)
        rows_ref[:, t * LANES : (t + 1) * LANES] = wide[j, pl.ds(h, count, 2), :].astype(BF)
    for i in range(ups):
        arrive(i)
        cols = slice(i * STEP_UP, (i + 1) * STEP_UP)
        hidden = dot(rows_ref[...], wo[cols, :], 1, 1)
        pg_ref[:, cols] = (hidden * slope[:, cols].astype(F32)).astype(BF)
    done, sent = set(), []
    for i in range(d // STEP_BACK):
        arrive(ups + i)
        back = dot(pg_ref[...], wi[i * STEP_BACK : (i + 1) * STEP_BACK, :], 1, 1)
        for u in range(STEP_BACK // LANES):
            t = i * (STEP_BACK // LANES) + u
            h, j = divmod(t, half_tiles)
            wide[j, pl.ds(h, count, 2), :] = back[:, u * LANES : (u + 1) * LANES]
            done.add(t)
            if {j, j + half_tiles} <= done:
                cols = slice(j * LANES, (j + 1) * LANES)
                out[:, cols] = wide[j].astype(BF)
                copy = pltpu.make_async_copy(
                    out.at[:, pl.ds(j * LANES, LANES)], out_hbm.at[:, pl.ds(j * LANES, LANES)], out_sems.at[j]
                )
                copy.start()
                sent.append(copy)
    for copy in sent:
        copy.wait()


def expert(x, w_out, w_in, slope):
    total, half = x.shape
    ff, d = w_out.shape
    raw = pl.BlockSpec(memory_space=pl.ANY)
    return pl.pallas_call(
        expert_kernel,
        in_specs=[WHOLE, raw, raw, raw],
        out_specs=raw,
        out_shape=pltpu.HBM((total, half), BF),
        scratch_shapes=[
            pltpu.VMEM((ff, d), BF),
            pltpu.VMEM((d, ff), BF),
            pltpu.VMEM(slope.shape, slope.dtype),
            pltpu.VMEM((total, half), BF),
            pltpu.VMEM((half // LANES, total, LANES), F32),
            pltpu.VMEM((total // 2, d), BF),
            pltpu.VMEM((total // 2, ff), BF),
            pltpu.SemaphoreType.DMA((ff // STEP_UP + d // STEP_BACK,)),
            pltpu.SemaphoreType.DMA((ff // STEP_UP,)),
            pltpu.SemaphoreType.DMA((half // LANES,)),
        ],
        compiler_params=pltpu.CompilerParams(vmem_limit_bytes=48 * MIB),
        cost_estimate=cost(2 * total * d * ff, 4 * ff * d + 2 * total * ff),
        name="expert",
    )(vmem(x), hbm(w_out), hbm(w_in), hbm(slope))


def back_kernel(
    y_ref, tok_hbm, disp_hbm, fc_hbm, lg_ref, sb_hbm, term_ref, wide, tok_ref, disp_ref, fc_ref, sb_ref, sems, sb_sems
):
    half_tiles, total, _ = wide.shape
    images, experts, d = sb_ref.shape
    stride = total // experts
    pairs = ((tok_hbm, tok_ref), (disp_hbm, disp_ref), (fc_hbm, fc_ref))
    copies = [
        [pltpu.make_async_copy(src.at[b], dst.at[b], sems.at[b, i]) for i, (src, dst) in enumerate(pairs)]
        for b in range(images)
    ]
    sb_copies = [pltpu.make_async_copy(sb_ref.at[b], sb_hbm.at[b], sb_sems.at[b]) for b in range(images)]
    for b in range(images):
        for copy in copies[b]:
            copy.start()
    for j in range(half_tiles):
        wide[j] = y_ref[:, j * LANES : (j + 1) * LANES].astype(F32)
    for b in range(images):
        for t in range(2 * half_tiles):
            h, j = divmod(t, half_tiles)
            sb_ref[b, :, t * LANES : (t + 1) * LANES] = wide[j, pl.ds(2 * b + h, experts, stride), :].astype(BF)
        sb_copies[b].start()
    term = jnp.zeros((experts, d), F32)
    for b in range(images):
        for copy in copies[b]:
            copy.wait()
        tok = tok_ref[b]
        disp = disp_ref[b]
        grad = dot(tok, sb_ref[b], 1, 1)
        from_dispatch = disp * (grad - jnp.sum(disp * grad, axis=0, keepdims=True))
        logit_grad = fc_ref[b] + from_dispatch
        lg_ref[b] = logit_grad.astype(BF)
        term = term + dot(logit_grad.T.astype(BF), tok, 1, 0)
    term_ref[...] = jnp.stack([term[:, : d // 2], term[:, d // 2 :]], axis=1).astype(BF)
    for copy in sb_copies:
        copy.wait()


def back(y, tokens, dispatch, from_combine):
    images, m, d = tokens.shape
    experts = dispatch.shape[2]
    total, half = y.shape
    raw = pl.BlockSpec(memory_space=pl.ANY)
    return pl.pallas_call(
        back_kernel,
        in_specs=[WHOLE, raw, raw, raw],
        out_specs=[WHOLE, raw, WHOLE],
        out_shape=[
            pltpu.VMEM((images, m, experts), BF),
            pltpu.HBM((images, experts, d), BF),
            pltpu.HBM((experts, 2, d // 2), BF),
        ],
        scratch_shapes=[
            pltpu.VMEM((half // LANES, total, LANES), F32),
            pltpu.VMEM((images, m, d), BF),
            pltpu.VMEM((images, m, experts), F32),
            pltpu.VMEM((images, m, experts), F32),
            pltpu.VMEM((images, experts, d), BF),
            pltpu.SemaphoreType.DMA((images, 3)),
            pltpu.SemaphoreType.DMA((images,)),
        ],
        compiler_params=pltpu.CompilerParams(vmem_limit_bytes=32 * MIB),
        cost_estimate=cost(4 * images * m * d * experts, 4 * images * m * d),
        name="back",
    )(vmem(y), hbm(tokens), hbm(dispatch), hbm(from_combine))


def token_kernel(disp_ref, lg_ref, sb_ref, router_t_ref, out_ref):
    b = pl.program_id(0)
    left = jnp.concatenate([disp_ref[0].astype(BF), lg_ref[b]], axis=1)
    right = jnp.concatenate([sb_ref[0], router_t_ref[...]], axis=0)
    out_ref[0] = dot(left, right, 1, 0).astype(BF)


def token_side(dispatch, logit_grad, slot_back, router_t):
    images, m, experts = dispatch.shape
    d = router_t.shape[1]
    return pl.pallas_call(
        token_kernel,
        grid=(images,),
        in_specs=[
            pl.BlockSpec((1, m, experts), lambda b: (b, 0, 0)),
            WHOLE,
            pl.BlockSpec((1, experts, d), lambda b: (b, 0, 0)),
            WHOLE,
        ],
        out_specs=pl.BlockSpec((1, m, d), lambda b: (b, 0, 0)),
        out_shape=pltpu.HBM((images, m, d), BF),
        compiler_params=pltpu.CompilerParams(vmem_limit_bytes=24 * MIB),
        cost_estimate=cost(4 * images * m * d * experts, 4 * images * m * d),
        name="token_side",
    )(hbm(dispatch), vmem(logit_grad), hbm(slot_back), vmem(router_t))


def sum_kernel(scale, x_ref, out_ref):
    devices = out_ref.shape[0]
    total = jnp.sum(x_ref[...].astype(F32), axis=0, keepdims=True) * scale
    out_ref[...] = jnp.broadcast_to(total, out_ref.shape).astype(BF)


def sum_terms(x, scale):
    return pl.pallas_call(
        functools.partial(sum_kernel, scale),
        in_specs=[WHOLE],
        out_specs=WHOLE,
        out_shape=pltpu.HBM(x.shape, BF),
        compiler_params=pltpu.CompilerParams(vmem_limit_bytes=24 * MIB),
        cost_estimate=cost(x.size, 4 * x.size),
        name="sum_terms",
    )(vmem(x))


def finish_kernel(x_ref, out_ref):
    half = x_ref.shape[2]
    wide = x_ref[...].astype(F32)
    for h in range(2):
        part = wide[:, h, :]
        for t in range(half // LANES):
            row = h * half + t * LANES
            out_ref[row : row + LANES, :] = part[:, t * LANES : (t + 1) * LANES].T


def finish(x):
    experts, two, half = x.shape
    return pl.pallas_call(
        finish_kernel,
        in_specs=[WHOLE],
        out_specs=WHOLE,
        out_shape=pltpu.HBM((two * half, experts), F32),
        compiler_params=pltpu.CompilerParams(vmem_limit_bytes=24 * MIB),
        cost_estimate=cost(x.size, 6 * x.size),
        name="finish",
    )(vmem(x))


def exchange(x):
    return lax.all_to_all(x, AXES, split_axis=0, concat_axis=0, tiled=True)


def exchange_rows(x, devices):
    rows, cols = x.shape
    return exchange(x.reshape(devices, rows // devices, cols)).reshape(rows, cols)


def local(tokens, router, cotangent, slot_out, pre_act, w_in, w_out):
    img_dev = tokens.shape[0]
    devices = lax.axis_size("dp") * lax.axis_size("expert")
    slot_grad, logits = front(tokens, router, cotangent)
    arrived = exchange_rows(slot_grad, devices)

    slope = gelu_slope(pre_act[0].astype(F32)).astype(BF)
    combine = jax.nn.softmax(logits, axis=2)
    dispatch = jax.nn.softmax(logits, axis=1)
    combine_grad = jnp.einsum("bmd,bed->bme", cotangent, slot_out, preferred_element_type=F32)
    from_combine = combine * (combine_grad - jnp.sum(combine * combine_grad, axis=2, keepdims=True))

    slot_back = expert(arrived, w_out[0], w_in[0], slope)
    returned = exchange_rows(slot_back, devices)
    logit_grad, slot_back, term = back(returned, tokens, dispatch, from_combine)
    terms = exchange(term)
    token_grad = token_side(dispatch, logit_grad, slot_back, router.T)
    gathered = exchange(sum_terms(terms, 1.0 / (img_dev * devices)))
    return token_grad, finish(gathered)


def solution(mesh):
    spec = P(AXES, None, None)
    return jax.shard_map(
        local,
        mesh=mesh,
        in_specs=(spec, P(), spec, spec, spec, spec, spec),
        out_specs=(spec, P()),
        check_vma=False,
    )
```

time: 134 us -> 121 us (0.903)
  local copies, waits for them, and re-layouts: 12.8 us -> 0.19 us
  Pallas kernels: 28 us -> 31.9 us
    unnamed x25 -> x5, local copies, waits for them, and re-layouts: 12.8 us -> 0.19 us
    add x1 -> x0, other arithmetic: 5.53 us -> none  [gelu_slope(): return normal_cdf + values * density]
    convert_element_type x0 -> x1, other arithmetic: none -> 4.51 us  [local(): slope = gelu_slope(pre_act[0].astype(F32)).astype(BF)]
    pallas_call x1, Pallas kernels: 3.41 us -> 6.64 us  [front(): pl.pallas_call(front_kernel, grid=(images,), in_specs=[pl.BlockSpec((1, m...]
    pallas_call x1, Pallas kernels: 2.72 us -> 4.49 us  [token_side(): pl.pallas_call(token_kernel, grid=(images,), in_specs=[pl.BlockSpec((1, m...]
  transfers between devices with their start and end apart: 3 -> 3, of which waited for: 3 -> 3; matrix products, arithmetic and copies ran while one was open for 11% -> 11% of each run, Pallas kernels for 2% -> 4%
where the time goes in v2:
time: 121 us
  waiting for transfers between devices  38.3 us (32%)
  Pallas kernels  31.9 us (26%)
  starting transfers between devices  19.6 us (16%)
  blocking collectives  16.7 us (14%)
  other arithmetic  8.37 us (7%)
  matrix products  4.85 us (4%)
    all_to_all x3, waiting for transfers between devices, exchange(): return lax.all_to_all(x, AXES, split_axis=0, concat_axis=0, tiled=True)  38.3 us
    all_to_all x3, starting transfers between devices, exchange(): return lax.all_to_all(x, AXES, split_axis=0, concat_axis=0, tiled=True)  19.6 us
    all_to_all x1, blocking collectives, exchange(): return lax.all_to_all(x, AXES, split_axis=0, concat_axis=0, tiled=True)  16.7 us
    pallas_call x1, Pallas kernels, expert(): pl.pallas_call(expert_kernel, in_specs=[WHOLE, raw, raw, raw], out_specs=...  12.8 us
    pallas_call x1, Pallas kernels, front(): pl.pallas_call(front_kernel, grid=(images,), in_specs=[pl.BlockSpec((1, m...  6.64 us
    pallas_call x1, Pallas kernels, back(): pl.pallas_call(back_kernel, in_specs=[WHOLE, raw, raw, raw], out_specs=[W...  5.62 us
    sub x1, matrix products, local(): combine_grad - jnp.sum(combine * combine_grad, axis=2, keepdims=True)  4.85 us
    convert_element_type x1, other arithmetic, local(): slope = gelu_slope(pre_act[0].astype(F32)).astype(BF)  4.51 us
  transfers between devices with their start and end apart: 3, of which 3 were waited for; matrix products, arithmetic and copies ran while one was open for 11% of the time, Pallas kernels for 4%

profile of v2, /device:TPU:1, one launch (start us, length us, event | category | flops | bytes accessed | tf_op | source)
XLA Modules:
  0.0 120.5 jit_solution(1109740292388961953)
XLA Ops:
  0.6 0.0 copy-start
  0.6 6.6 %front.1 = (bf16[1024,640]{1,0:T(8,128)(2,1)}, f32[4,256,128]{2,1,0:T(8,128)}) custom-call(bf16[4,256,1280]{2,1,0:T(8,128)(2,1)} %tok_hbm.1, bf16[1280,128]{1,0:T(8,128)(2,1)} %router_ref.1, bf16[4,256,1280]{2,1,0:T(8,128)(2,1)} %cot_ref.1), custom_call_target="tpu_custom_call" | custom-call | flops 671088640 | bytes 10485760 | tf_op jit(solution)/shard_map/front/pallas_call | solution.py:72
  7.3 11.5 %all-to-all-start = ((bf16[128,8,640]{2,1,0:T(8,128)(2,1)}), bf16[128,8,640]{2,1,0:T(8,128)(2,1)S(1)}, u32[]{:S(2)}, u32[]{:S(2)}) async-start(bf16[128,8,640]{2,1,0:T(8,128)(2,1)} %bitcast.20), calls=%async_computation | async-start | bytes 2621440 | tf_op jit(solution)/shard_map/all_to_all | solution.py:320
  18.8 4.5 %fusion.11.slope_hbm = bf16[512,2560]{1,0:T(8,128)(2,1)} fusion(bf16[1,512,2560]{2,1,0:T(8,128)(2,1)} %param.11), kind=kLoop, calls=%fused_computation.15 | loop fusion | flops 13107200 | bytes 5242880 | tf_op jit(solution)/shard_map/convert_element_type | solution.py:334
  23.3 17.4 %all-to-all-done = bf16[128,8,640]{2,1,0:T(8,128)(2,1)S(1)} async-done(((bf16[128,8,640]{2,1,0:T(8,128)(2,1)}), bf16[128,8,640]{2,1,0:T(8,128)(2,1)S(1)}, u32[]{:S(2)}, u32[]{:S(2)}) %all-to-all-start) | async-done | bytes 1310752 | tf_op jit(solution)/shard_map/all_to_all | solution.py:320
  40.7 12.8 %expert.1 = bf16[1024,640]{1,0:T(8,128)(2,1)} custom-call(bf16[1024,640]{1,0:T(8,128)(2,1)S(1)} %bitcast.18, bf16[2560,1280]{1,0:T(8,128)(2,1)} %bitcast.21, bf16[1280,2560]{1,0:T(8,128)(2,1)} %bitcast.22, bf16[512,2560]{1,0:T(8,128)(2,1)} %fusion.11.slope_hbm), custom_call_target="tpu_custom_call" | custom-call | flops 6710886400 | bytes 18350080 | tf_op jit(solution)/shard_map/expert/pallas_call | solution.py:161
  53.5 4.3 %all-to-all-start.1 = ((bf16[128,8,640]{2,1,0:T(8,128)(2,1)}), bf16[128,8,640]{2,1,0:T(8,128)(2,1)S(1)}, u32[]{:S(2)}, u32[]{:S(2)}) async-start(bf16[128,8,640]{2,1,0:T(8,128)(2,1)} %bitcast.19), calls=%async_computation.1 | async-start | bytes 2621440 | tf_op jit(solution)/shard_map/all_to_all | solution.py:320
  57.8 2.3 %fusion.13.disp_hbm.disp_ref = f32[4,256,128]{2,1,0:T(8,128)} fusion(f32[4,256,128]{2,1,0:T(8,128)} %get-tuple-element.7), kind=kOutput, calls=%fused_computation.17 | output fusion | flops 263678 | bytes 1048576 | tf_op jit(solution)/shard_map/div | solution.py:336
  60.0 1.6 %fusion.15 = f32[4,256,128]{2,1,0:T(8,128)S(1)} fusion(f32[4,256,128]{2,1,0:T(8,128)} %get-tuple-element.7), kind=kOutput, calls=%fused_computation.19 | output fusion | flops 264446 | bytes 1048576 | tf_op jit(solution)/shard_map/div | solution.py:335
  61.6 0.0 copy-done
  61.6 4.9 %fusion.19.fc_hbm = f32[4,256,128]{2,1,0:T(8,128)} fusion(f32[4,256,128]{2,1,0:T(8,128)S(1)} %fusion.15, bf16[4,256,1280]{2,1,0:T(8,128)(2,1)} %cot_ref.1, bf16[4,128,1280]{2,1,0:T(8,128)(2,1)S(1)} %copy-done), kind=kOutput, calls=%fused_computation.23 | convolution fusion | flops 671483008 | bytes 4980736 | tf_op jit(solution)/shard_map/sub | solution.py:338
  66.5 13.4 %all-to-all-done.1 = bf16[128,8,640]{2,1,0:T(8,128)(2,1)S(1)} async-done(((bf16[128,8,640]{2,1,0:T(8,128)(2,1)}), bf16[128,8,640]{2,1,0:T(8,128)(2,1)S(1)}, u32[]{:S(2)}, u32[]{:S(2)}) %all-to-all-start.1) | async-done | bytes 1310752 | tf_op jit(solution)/shard_map/all_to_all | solution.py:320
  79.9 0.0 copy-start.1
  79.9 5.6 %back.1 = (bf16[4,256,128]{2,1,0:T(8,128)(2,1)S(1)}, bf16[4,128,1280]{2,1,0:T(8,128)(2,1)}, bf16[128,2,640]{2,1,0:T(2,128)(2,1)}) custom-call(bf16[1024,640]{1,0:T(8,128)(2,1)S(1)} %bitcast.16, bf16[4,256,1280]{2,1,0:T(8,128)(2,1)} %tok_hbm.1, f32[4,256,128]{2,1,0:T(8,128)} %fusion.13.disp_hbm.disp_ref, f32[4,256,128]{2,1,0:T(8,128)} %fusion.19.fc_hbm), custom_call_target="tpu_custom_call" | custom-call | flops 671088640 | bytes 5242880 | tf_op jit(solution)/shard_map/back/pallas_call | solution.py:227
  85.5 16.7 %all_to_all.20.x_ref = bf16[128,2,640]{2,1,0:T(2,128)(2,1)S(1)} all-to-all(bf16[128,2,640]{2,1,0:T(2,128)(2,1)} %get-tuple-element.11), channel_id=1, replica_groups=mesh['dp'=8,'expert'=16] {'dp','expert'}, dimensions={0} | all-to-all | bytes 655360 | tf_op jit(solution)/shard_map/all_to_all | solution.py:320
  102.2 1.1 sum_terms.1
  103.3 3.9 %all-to-all-start.3 = ((bf16[128,2,640]{2,1,0:T(2,128)(2,1)}), bf16[128,2,640]{2,1,0:T(2,128)(2,1)S(1)}, u32[]{:S(2)}, u32[]{:S(2)}) async-start(bf16[128,2,640]{2,1,0:T(2,128)(2,1)} %sum_terms.1), calls=%async_computation.3 | async-start | bytes 655360 | tf_op jit(solution)/shard_map/all_to_all | solution.py:320
  107.2 0.0 copy-done.1
  107.2 0.2 copy.11
  107.4 4.5 %token_side.1 = bf16[4,256,1280]{2,1,0:T(8,128)(2,1)} custom-call(f32[4,256,128]{2,1,0:T(8,128)} %fusion.13.disp_hbm.disp_ref, bf16[4,256,128]{2,1,0:T(8,128)(2,1)S(1)} %get-tuple-element.9.lg_ref, bf16[4,128,1280]{2,1,0:T(8,128)(2,1)} %get-tuple-element.10.sb_ref, bf16[128,1280]{1,0:T(8,128)(2,1)S(1)} %bitcast.17), custom_call_target="tpu_custom_call" | custom-call | flops 671088640 | bytes 5242880 | tf_op jit(solution)/shard_map/token_side/pallas_call | solution.py:261
  111.9 7.4 %all-to-all-done.3.x_ref = bf16[128,2,640]{2,1,0:T(2,128)(2,1)S(1)} async-done(((bf16[128,2,640]{2,1,0:T(2,128)(2,1)}), bf16[128,2,640]{2,1,0:T(2,128)(2,1)S(1)}, u32[]{:S(2)}, u32[]{:S(2)}) %all-to-all-start.3) | async-done | bytes 327712 | tf_op jit(solution)/shard_map/all_to_all | solution.py:320
  119.3 1.2 %finish.1 = f32[1280,128]{1,0:T(8,128)} custom-call(bf16[128,2,640]{2,1,0:T(2,128)(2,1)S(1)} %all-to-all-done.3.x_ref), custom_call_target="tpu_custom_call" | custom-call | flops 163840 | bytes 983040 | tf_op jit(solution)/shard_map/finish/pallas_call | solution.py:308
Async XLA Ops:
  0.6 61.0 %copy-start = (bf16[4,128,1280]{2,1,0:T(8,128)(2,1)S(1)}, bf16[4,128,1280]{2,1,0:T(8,128)(2,1)}, u32[]{:S(2)}) copy-start(bf16[4,128,1280]{2,1,0:T(8,128)(2,1)} %param.10) | copy-start | bytes 3932164
  7.3 33.5 %all-to-all-start = ((bf16[128,8,640]{2,1,0:T(8,128)(2,1)}), bf16[128,8,640]{2,1,0:T(8,128)(2,1)S(1)}, u32[]{:S(2)}, u32[]{:S(2)}) async-start(bf16[128,8,640]{2,1,0:T(8,128)(2,1)} %bitcast.20), calls=%async_computation | async-start | bytes 2621440 | tf_op jit(solution)/shard_map/all_to_all | solution.py:320
  53.5 26.4 %all-to-all-start.1 = ((bf16[128,8,640]{2,1,0:T(8,128)(2,1)}), bf16[128,8,640]{2,1,0:T(8,128)(2,1)S(1)}, u32[]{:S(2)}, u32[]{:S(2)}) async-start(bf16[128,8,640]{2,1,0:T(8,128)(2,1)} %bitcast.19), calls=%async_computation.1 | async-start | bytes 2621440 | tf_op jit(solution)/shard_map/all_to_all | solution.py:320
  79.9 27.3 %copy-start.1 = (bf16[1280,128]{1,0:T(8,128)(2,1)S(1)}, bf16[1280,128]{1,0:T(8,128)(2,1)}, u32[]{:S(2)}) copy-start(bf16[1280,128]{1,0:T(8,128)(2,1)} %router_ref.1) | copy-start | bytes 983044
  103.3 16.0 %all-to-all-start.3 = ((bf16[128,2,640]{2,1,0:T(2,128)(2,1)}), bf16[128,2,640]{2,1,0:T(2,128)(2,1)S(1)}, u32[]{:S(2)}, u32[]{:S(2)}) async-start(bf16[128,2,640]{2,1,0:T(2,128)(2,1)} %sum_terms.1), calls=%async_computation.3 | async-start | bytes 655360 | tf_op jit(solution)/shard_map/all_to_all | solution.py:320

commit v3 on v2

--- a/solution.py
+++ b/solution.py
@@ -45,71 +45,98 @@
     return e / jnp.sum(e, axis=axis, keepdims=True)
 
 
-def front_kernel(tok_ref, router_ref, cot_ref, sg_ref, logits_ref, rows):
-    b = pl.program_id(0)
-    n = pl.num_programs(0)
-    logits = dot(tok_ref[0], router_ref[...], 1, 0)
-    logits_ref[0] = logits
-    combine = softmax(logits, 1).astype(BF)
-    slot_grad = dot(combine, cot_ref[0], 0, 0)
-    half_tiles = rows.shape[0]
-    experts = slot_grad.shape[0]
-    stride = rows.shape[1] // experts
-    for t in range(2 * half_tiles):
-        h, j = divmod(t, half_tiles)
-        rows[j, pl.ds(2 * b + h, experts, stride), :] = slot_grad[:, t * LANES : (t + 1) * LANES]
-
-    @pl.when(b == n - 1)
-    def _():
-        for j in range(half_tiles):
-            sg_ref[:, j * LANES : (j + 1) * LANES] = rows[j].astype(BF)
+def front_kernel(
+    tok_hbm, router_hbm, cot_hbm, sg_hbm, logits_hbm, router, tok, cot, sg, logits_ref, combine, rows, in_sems, l_sem, o_sems
+):
+    images = tok.shape[0]
+    half_tiles, total, _ = rows.shape
+    experts = router.shape[1]
+    stride = total // experts
+    pairs = ((router_hbm, router), (tok_hbm, tok), (cot_hbm, cot))
+    router_copy, tok_copy, cot_copy = [
+        pltpu.make_async_copy(src, dst, in_sems.at[i]) for i, (src, dst) in enumerate(pairs)
+    ]
+    for copy in (router_copy, tok_copy, cot_copy):
+        copy.start()
+    router_copy.wait()
+    tok_copy.wait()
+    for b in range(images):
+        logits = dot(tok[b], router[...], 1, 0)
+        logits_ref[b] = logits
+        combine[b] = softmax(logits, 1).astype(BF)
+    sent = [pltpu.make_async_copy(logits_ref, logits_hbm, l_sem)]
+    sent[0].start()
+    cot_copy.wait()
+    for b in range(images):
+        slot_grad = dot(combine[b], cot[b], 0, 0)
+        for t in range(2 * half_tiles):
+            h, j = divmod(t, half_tiles)
+            rows[j, pl.ds(2 * b + h, experts, stride), :] = slot_grad[:, t * LANES : (t + 1) * LANES]
+    for j in range(half_tiles):
+        sg[:, j * LANES : (j + 1) * LANES] = rows[j].astype(BF)
+        cols = pl.ds(j * LANES, LANES)
+        sent.append(pltpu.make_async_copy(sg.at[:, cols], sg_hbm.at[:, cols], o_sems.at[j]))
+        sent[-1].start()
+    for copy in sent:
+        copy.wait()
 
 
 def front(tokens, router, cotangent):
     images, m, d = tokens.shape
     experts = router.shape[1]
     total = experts * images * 2
+    half_tiles = d // 2 // LANES
+    raw = pl.BlockSpec(memory_space=pl.ANY)
     return pl.pallas_call(
         front_kernel,
-        grid=(images,),
-        in_specs=[
-            pl.BlockSpec((1, m, d), lambda b: (b, 0, 0)),
-            pl.BlockSpec((d, experts), lambda b: (0, 0)),
-            pl.BlockSpec((1, m, d), lambda b: (b, 0, 0)),
-        ],
-        out_specs=[
-            pl.BlockSpec((total, d // 2), lambda b: (0, 0)),
-            pl.BlockSpec((1, m, experts), lambda b: (b, 0, 0)),
-        ],
+        in_specs=[raw] * 3,
+        out_specs=[raw] * 2,
         out_shape=[
             pltpu.HBM((total, d // 2), BF),
             pltpu.HBM((images, m, experts), F32),
         ],
-        scratch_shapes=[pltpu.VMEM((d // 2 // LANES, total, LANES), F32)],
-        compiler_params=pltpu.CompilerParams(vmem_limit_bytes=24 * MIB),
+        scratch_shapes=[
+            pltpu.VMEM(router.shape, BF),
+            pltpu.VMEM(tokens.shape, BF),
+            pltpu.VMEM(tokens.shape, BF),
+            pltpu.VMEM((total, d // 2), BF),
+            pltpu.VMEM((images, m, experts), F32),
+            pltpu.VMEM((images, m, experts), BF),
+            pltpu.VMEM((half_tiles, total, LANES), F32),
+            pltpu.SemaphoreType.DMA((3,)),
+            pltpu.SemaphoreType.DMA(()),
+            pltpu.SemaphoreType.DMA((half_tiles,)),
+        ],
+        compiler_params=pltpu.CompilerParams(vmem_limit_bytes=32 * MIB),
         cost_estimate=cost(4 * images * m * d * experts, 4 * images * m * d + 4 * total * d),
         name="front",
     )(hbm(tokens), hbm(router), hbm(cotangent))
 
 
-STEP_UP = 512
-STEP_BACK = 640
-WINDOW = 3
+UP_CUTS = (0, 1024, 2560)
+BACK_CUTS = (0, 1280)
+WINDOW = 2
+
+
+def spans(cuts, size):
+    return [(lo * size // cuts[-1], hi * size // cuts[-1]) for lo, hi in zip(cuts, cuts[1:])]
 
 
 def expert_kernel(x_ref, wo_hbm, wi_hbm, slope_hbm, out_hbm, wo, wi, slope, out, wide, rows_ref, pg_ref, w_sems, slope_sems, out_sems):
     half_tiles, total, _ = wide.shape
     count = total // 2
     ff, d = wo.shape
-    pieces = [(wo_hbm, wo, pl.ds(c, STEP_UP)) for c in range(0, ff, STEP_UP)]
-    ups = len(pieces)
-    pieces += [(wi_hbm, wi, pl.ds(c, STEP_BACK)) for c in range(0, d, STEP_BACK)]
-    groups = [
-        [pltpu.make_async_copy(src.at[r], dst.at[r], w_sems.at[i])] for i, (src, dst, r) in enumerate(pieces)
-    ]
-    for i in range(ups):
-        cols = pl.ds(i * STEP_UP, STEP_UP)
-        groups[i].append(pltpu.make_async_copy(slope_hbm.at[:, cols], slope.at[:, cols], slope_sems.at[i]))
+    ups, backs = spans(UP_CUTS, ff), spans(BACK_CUTS, d)
+    groups = []
+    for i, (lo, hi) in enumerate(ups):
+        cut = pl.ds(lo, hi - lo)
+        groups.append([
+            pltpu.make_async_copy(wo_hbm.at[cut], wo.at[cut], w_sems.at[i]),
+            pltpu.make_async_copy(slope_hbm.at[:, cut], slope.at[:, cut], slope_sems.at[i]),
+        ])
+    for i, (lo, hi) in enumerate(backs):
+        cut = pl.ds(lo, hi - lo)
+        groups.append([pltpu.make_async_copy(wi_hbm.at[cut], wi.at[cut], w_sems.at[len(ups) + i])])
 
     def start(i):
         for copy in groups[i]:
@@ -128,19 +155,18 @@
     for t in range(2 * half_tiles):
         h, j = divmod(t, half_tiles)
         rows_ref[:, t * LANES : (t + 1) * LANES] = wide[j, pl.ds(h, count, 2), :].astype(BF)
-    for i in range(ups):
+    for i, (lo, hi) in enumerate(ups):
         arrive(i)
-        cols = slice(i * STEP_UP, (i + 1) * STEP_UP)
-        hidden = dot(rows_ref[...], wo[cols, :], 1, 1)
-        pg_ref[:, cols] = (hidden * slope[:, cols].astype(F32)).astype(BF)
+        hidden = dot(rows_ref[...], wo[lo:hi, :], 1, 1)
+        pg_ref[:, lo:hi] = (hidden * slope[:, lo:hi]).astype(BF)
     done, sent = set(), []
-    for i in range(d // STEP_BACK):
-        arrive(ups + i)
-        back = dot(pg_ref[...], wi[i * STEP_BACK : (i + 1) * STEP_BACK, :], 1, 1)
-        for u in range(STEP_BACK // LANES):
-            t = i * (STEP_BACK // LANES) + u
+    for i, (lo, hi) in enumerate(backs):
+        arrive(len(ups) + i)
+        back = dot(pg_ref[...], wi[lo:hi, :], 1, 1)
+        for t in range(lo // LANES, hi // LANES):
             h, j = divmod(t, half_tiles)
-            wide[j, pl.ds(h, count, 2), :] = back[:, u * LANES : (u + 1) * LANES]
+            at = t * LANES - lo
+            wide[j, pl.ds(h, count, 2), :] = back[:, at : at + LANES]
             done.add(t)
             if {j, j + half_tiles} <= done:
                 cols = slice(j * LANES, (j + 1) * LANES)
@@ -171,52 +197,50 @@
             pltpu.VMEM((half // LANES, total, LANES), F32),
             pltpu.VMEM((total // 2, d), BF),
             pltpu.VMEM((total // 2, ff), BF),
-            pltpu.SemaphoreType.DMA((ff // STEP_UP + d // STEP_BACK,)),
-            pltpu.SemaphoreType.DMA((ff // STEP_UP,)),
+            pltpu.SemaphoreType.DMA((len(UP_CUTS) + len(BACK_CUTS) - 2,)),
+            pltpu.SemaphoreType.DMA((len(UP_CUTS) - 1,)),
             pltpu.SemaphoreType.DMA((half // LANES,)),
         ],
-        compiler_params=pltpu.CompilerParams(vmem_limit_bytes=48 * MIB),
+        compiler_params=pltpu.CompilerParams(vmem_limit_bytes=56 * MIB),
         cost_estimate=cost(2 * total * d * ff, 4 * ff * d + 2 * total * ff),
         name="expert",
     )(vmem(x), hbm(w_out), hbm(w_in), hbm(slope))
 
 
 def back_kernel(
-    y_ref, tok_hbm, disp_hbm, fc_hbm, lg_ref, sb_hbm, term_ref, wide, tok_ref, disp_ref, fc_ref, sb_ref, sems, sb_sems
+    y_ref, tok_hbm, disp_hbm, fc_hbm, lg_ref, sb_hbm, term_hbm, wide, tok, disp, fc, sb, lg_t, term_ref, in_sems, out_sems
 ):
     half_tiles, total, _ = wide.shape
-    images, experts, d = sb_ref.shape
+    images, experts, d = sb.shape
+    m = tok.shape[1]
     stride = total // experts
-    pairs = ((tok_hbm, tok_ref), (disp_hbm, disp_ref), (fc_hbm, fc_ref))
-    copies = [
-        [pltpu.make_async_copy(src.at[b], dst.at[b], sems.at[b, i]) for i, (src, dst) in enumerate(pairs)]
-        for b in range(images)
-    ]
-    sb_copies = [pltpu.make_async_copy(sb_ref.at[b], sb_hbm.at[b], sb_sems.at[b]) for b in range(images)]
-    for b in range(images):
-        for copy in copies[b]:
-            copy.start()
+    pairs = ((tok_hbm, tok), (disp_hbm, disp), (fc_hbm, fc))
+    arrivals = [pltpu.make_async_copy(src, dst, in_sems.at[i]) for i, (src, dst) in enumerate(pairs)]
+    for copy in arrivals:
+        copy.start()
     for j in range(half_tiles):
         wide[j] = y_ref[:, j * LANES : (j + 1) * LANES].astype(F32)
     for b in range(images):
         for t in range(2 * half_tiles):
             h, j = divmod(t, half_tiles)
-            sb_ref[b, :, t * LANES : (t + 1) * LANES] = wide[j, pl.ds(2 * b + h, experts, stride), :].astype(BF)
-        sb_copies[b].start()
-    term = jnp.zeros((experts, d), F32)
+            sb[b, :, t * LANES : (t + 1) * LANES] = wide[j, pl.ds(2 * b + h, experts, stride), :].astype(BF)
+    for copy in arrivals:
+        copy.wait()
     for b in range(images):
-        for copy in copies[b]:
-            copy.wait()
-        tok = tok_ref[b]
-        disp = disp_ref[b]
-        grad = dot(tok, sb_ref[b], 1, 1)
-        from_dispatch = disp * (grad - jnp.sum(disp * grad, axis=0, keepdims=True))
-        logit_grad = fc_ref[b] + from_dispatch
+        grad = dot(tok[b], sb[b], 1, 1)
+        from_dispatch = disp[b] * (grad - jnp.sum(disp[b] * grad, axis=0, keepdims=True))
+        logit_grad = fc[b] + from_dispatch
         lg_ref[b] = logit_grad.astype(BF)
-        term = term + dot(logit_grad.T.astype(BF), tok, 1, 0)
-    term_ref[...] = jnp.stack([term[:, : d // 2], term[:, d // 2 :]], axis=1).astype(BF)
-    for copy in sb_copies:
-        copy.wait()
+        lg_t[:, b * m : (b + 1) * m] = logit_grad.T.astype(BF)
+    sb_copy = pltpu.make_async_copy(sb, sb_hbm, out_sems.at[0])
+    sb_copy.start()
+    term = dot(lg_t[...], tok[...].reshape(images * m, d), 1, 0)
+    for h in range(2):
+        term_ref[:, h, :] = term[:, h * (d // 2) : (h + 1) * (d // 2)].astype(BF)
+    term_copy = pltpu.make_async_copy(term_ref, term_hbm, out_sems.at[1])
+    term_copy.start()
+    sb_copy.wait()
+    term_copy.wait()
 
 
 def back(y, tokens, dispatch, from_combine):
@@ -227,7 +251,7 @@
     return pl.pallas_call(
         back_kernel,
         in_specs=[WHOLE, raw, raw, raw],
-        out_specs=[WHOLE, raw, WHOLE],
+        out_specs=[WHOLE, raw, raw],
         out_shape=[
             pltpu.VMEM((images, m, experts), BF),
             pltpu.HBM((images, experts, d), BF),
@@ -239,8 +263,10 @@
             pltpu.VMEM((images, m, experts), F32),
             pltpu.VMEM((images, m, experts), F32),
             pltpu.VMEM((images, experts, d), BF),
-            pltpu.SemaphoreType.DMA((images, 3)),
-            pltpu.SemaphoreType.DMA((images,)),
+            pltpu.VMEM((experts, images * m), BF),
+            pltpu.VMEM((experts, 2, d // 2), BF),
+            pltpu.SemaphoreType.DMA((3,)),
+            pltpu.SemaphoreType.DMA((2,)),
         ],
         compiler_params=pltpu.CompilerParams(vmem_limit_bytes=32 * MIB),
         cost_estimate=cost(4 * images * m * d * experts, 4 * images * m * d),
@@ -276,9 +302,12 @@
 
 
 def sum_kernel(scale, x_ref, out_ref):
-    devices = out_ref.shape[0]
-    total = jnp.sum(x_ref[...].astype(F32), axis=0, keepdims=True) * scale
-    out_ref[...] = jnp.broadcast_to(total, out_ref.shape).astype(BF)
+    step = 8
+    part = x_ref[:step].astype(F32)
+    for i in range(step, x_ref.shape[0], step):
+        part = part + x_ref[i : i + step].astype(F32)
+    total = jnp.sum(part, axis=0, keepdims=True) * scale
+    out_ref[...] = jnp.broadcast_to(total.astype(BF), out_ref.shape)
 
 
 def sum_terms(x, scale):
@@ -331,7 +360,7 @@
     slot_grad, logits = front(tokens, router, cotangent)
     arrived = exchange_rows(slot_grad, devices)
 
-    slope = gelu_slope(pre_act[0].astype(F32)).astype(BF)
+    slope = gelu_slope(pre_act[0].astype(F32))
     combine = jax.nn.softmax(logits, axis=2)
     dispatch = jax.nn.softmax(logits, axis=1)
     combine_grad = jnp.einsum("bmd,bed->bme", cotangent, slot_out, preferred_element_type=F32)

time: 121 us -> 117 us (0.967)
  Pallas kernels: 31.9 us -> 28.1 us
    add x0 -> x1, other arithmetic: none -> 5.58 us  [gelu_slope(): return normal_cdf + values * density]
    convert_element_type x1 -> x0, other arithmetic: 4.51 us -> none  [local(): slope = gelu_slope(pre_act[0].astype(F32)).astype(BF)]
    pallas_call x1, Pallas kernels: 6.64 us -> 5.01 us  [front(): pl.pallas_call(front_kernel, in_specs=[raw] * 3, out_specs=[raw] * 2, out...]
    pallas_call x1, Pallas kernels: 5.62 us -> 4.33 us  [back(): pl.pallas_call(back_kernel, in_specs=[WHOLE, raw, raw, raw], out_specs=[W...]
  transfers between devices with their start and end apart: 3 -> 3, of which waited for: 3 -> 3; matrix products, arithmetic and copies ran while one was open for 11% -> 12% of each run, Pallas kernels for 4% -> 4%
where the time goes in v3:
time: 117 us
  waiting for transfers between devices  37.1 us (32%)
  Pallas kernels  28.1 us (24%)
  starting transfers between devices  19.6 us (17%)
  blocking collectives  16.7 us (14%)
  other arithmetic  9.51 us (8%)
  matrix products  4.84 us (4%)
    all_to_all x3, waiting for transfers between devices, exchange(): return lax.all_to_all(x, AXES, split_axis=0, concat_axis=0, tiled=True)  37.1 us
    all_to_all x3, starting transfers between devices, exchange(): return lax.all_to_all(x, AXES, split_axis=0, concat_axis=0, tiled=True)  19.6 us
    all_to_all x1, blocking collectives, exchange(): return lax.all_to_all(x, AXES, split_axis=0, concat_axis=0, tiled=True)  16.7 us
    pallas_call x1, Pallas kernels, expert(): pl.pallas_call(expert_kernel, in_specs=[WHOLE, raw, raw, raw], out_specs=...  12.2 us
    add x1, other arithmetic, gelu_slope(): return normal_cdf + values * density  5.58 us
    pallas_call x1, Pallas kernels, front(): pl.pallas_call(front_kernel, in_specs=[raw] * 3, out_specs=[raw] * 2, out...  5.01 us
    sub x1, matrix products, local(): combine_grad - jnp.sum(combine * combine_grad, axis=2, keepdims=True)  4.84 us
    pallas_call x1, Pallas kernels, token_side(): pl.pallas_call(token_kernel, grid=(images,), in_specs=[pl.BlockSpec((1, m...  4.49 us
  transfers between devices with their start and end apart: 3, of which 3 were waited for; matrix products, arithmetic and copies ran while one was open for 12% of the time, Pallas kernels for 4%

profile of v3, /device:TPU:1, one launch (start us, length us, event | category | flops | bytes accessed | tf_op | source)
XLA Modules:
  0.0 116.8 jit_solution(369804444437702574)
XLA Ops:
  0.6 0.0 copy-start
  0.6 5.0 %front.1 = (bf16[1024,640]{1,0:T(8,128)(2,1)}, f32[4,256,128]{2,1,0:T(8,128)}) custom-call(bf16[4,256,1280]{2,1,0:T(8,128)(2,1)} %tok_hbm.3, bf16[1280,128]{1,0:T(8,128)(2,1)} %router_hbm.1, bf16[4,256,1280]{2,1,0:T(8,128)(2,1)} %cot_hbm.1), custom_call_target="tpu_custom_call" | custom-call | flops 671088640 | bytes 10485760 | tf_op jit(solution)/shard_map/front/pallas_call | solution.py:90
  5.7 11.5 %all-to-all-start = ((bf16[128,8,640]{2,1,0:T(8,128)(2,1)}), bf16[128,8,640]{2,1,0:T(8,128)(2,1)S(1)}, u32[]{:S(2)}, u32[]{:S(2)}) async-start(bf16[128,8,640]{2,1,0:T(8,128)(2,1)} %bitcast.20), calls=%async_computation | async-start | bytes 2621440 | tf_op jit(solution)/shard_map/all_to_all | solution.py:349
  17.2 5.6 %fusion.8.slope_hbm = f32[512,2560]{1,0:T(8,128)} fusion(bf16[1,512,2560]{2,1,0:T(8,128)(2,1)} %param.11), kind=kLoop, calls=%fused_computation.12 | loop fusion | flops 11796480 | bytes 7864320 | tf_op jit(solution)/shard_map/add | solution.py:36
  22.7 16.4 %all-to-all-done = bf16[128,8,640]{2,1,0:T(8,128)(2,1)S(1)} async-done(((bf16[128,8,640]{2,1,0:T(8,128)(2,1)}), bf16[128,8,640]{2,1,0:T(8,128)(2,1)S(1)}, u32[]{:S(2)}, u32[]{:S(2)}) %all-to-all-start) | async-done | bytes 1310752 | tf_op jit(solution)/shard_map/all_to_all | solution.py:349
  39.1 12.2 %expert.1 = bf16[1024,640]{1,0:T(8,128)(2,1)} custom-call(bf16[1024,640]{1,0:T(8,128)(2,1)S(1)} %bitcast.18, bf16[2560,1280]{1,0:T(8,128)(2,1)} %bitcast.21, bf16[1280,2560]{1,0:T(8,128)(2,1)} %bitcast.22, f32[512,2560]{1,0:T(8,128)} %fusion.8.slope_hbm), custom_call_target="tpu_custom_call" | custom-call | flops 6710886400 | bytes 18350080 | tf_op jit(solution)/shard_map/expert/pallas_call | solution.py:187
  51.3 4.3 %all-to-all-start.1 = ((bf16[128,8,640]{2,1,0:T(8,128)(2,1)}), bf16[128,8,640]{2,1,0:T(8,128)(2,1)S(1)}, u32[]{:S(2)}, u32[]{:S(2)}) async-start(bf16[128,8,640]{2,1,0:T(8,128)(2,1)} %bitcast.19), calls=%async_computation.1 | async-start | bytes 2621440 | tf_op jit(solution)/shard_map/all_to_all | solution.py:349
  55.6 2.3 %fusion.12.disp_hbm.disp_ref = f32[4,256,128]{2,1,0:T(8,128)} fusion(f32[4,256,128]{2,1,0:T(8,128)} %get-tuple-element.7), kind=kOutput, calls=%fused_computation.16 | output fusion | flops 263678 | bytes 1048576 | tf_op jit(solution)/shard_map/div | solution.py:365
  57.9 1.6 %fusion.14 = f32[4,256,128]{2,1,0:T(8,128)S(1)} fusion(f32[4,256,128]{2,1,0:T(8,128)} %get-tuple-element.7), kind=kOutput, calls=%fused_computation.18 | output fusion | flops 264446 | bytes 1048576 | tf_op jit(solution)/shard_map/div | solution.py:364
  59.5 0.0 copy-done
  59.5 4.8 %fusion.18.fc_hbm = f32[4,256,128]{2,1,0:T(8,128)} fusion(f32[4,256,128]{2,1,0:T(8,128)S(1)} %fusion.14, bf16[4,256,1280]{2,1,0:T(8,128)(2,1)} %cot_hbm.1, bf16[4,128,1280]{2,1,0:T(8,128)(2,1)S(1)} %copy-done), kind=kOutput, calls=%fused_computation.22 | convolution fusion | flops 671483008 | bytes 4980736 | tf_op jit(solution)/shard_map/sub | solution.py:367
  64.4 13.3 %all-to-all-done.1 = bf16[128,8,640]{2,1,0:T(8,128)(2,1)S(1)} async-done(((bf16[128,8,640]{2,1,0:T(8,128)(2,1)}), bf16[128,8,640]{2,1,0:T(8,128)(2,1)S(1)}, u32[]{:S(2)}, u32[]{:S(2)}) %all-to-all-start.1) | async-done | bytes 1310752 | tf_op jit(solution)/shard_map/all_to_all | solution.py:349
  77.7 0.0 copy-start.1
  77.7 4.3 %back.1 = (bf16[4,256,128]{2,1,0:T(8,128)(2,1)S(1)}, bf16[4,128,1280]{2,1,0:T(8,128)(2,1)}, bf16[128,2,640]{2,1,0:T(2,128)(2,1)}) custom-call(bf16[1024,640]{1,0:T(8,128)(2,1)S(1)} %bitcast.16, bf16[4,256,1280]{2,1,0:T(8,128)(2,1)} %tok_hbm.3, f32[4,256,128]{2,1,0:T(8,128)} %fusion.12.disp_hbm.disp_ref, f32[4,256,128]{2,1,0:T(8,128)} %fusion.18.fc_hbm), custom_call_target="tpu_custom_call" | custom-call | flops 671088640 | bytes 5242880 | tf_op jit(solution)/shard_map/back/pallas_call | solution.py:251
  82.0 16.7 %all_to_all.20.x_ref = bf16[128,2,640]{2,1,0:T(2,128)(2,1)S(1)} all-to-all(bf16[128,2,640]{2,1,0:T(2,128)(2,1)} %get-tuple-element.11), channel_id=1, replica_groups=mesh['dp'=8,'expert'=16] {'dp','expert'}, dimensions={0} | all-to-all | bytes 655360 | tf_op jit(solution)/shard_map/all_to_all | solution.py:349
  98.7 0.8 sum_terms.1
  99.5 3.9 %all-to-all-start.3 = ((bf16[128,2,640]{2,1,0:T(2,128)(2,1)}), bf16[128,2,640]{2,1,0:T(2,128)(2,1)S(1)}, u32[]{:S(2)}, u32[]{:S(2)}) async-start(bf16[128,2,640]{2,1,0:T(2,128)(2,1)} %sum_terms.1), calls=%async_computation.3 | async-start | bytes 655360 | tf_op jit(solution)/shard_map/all_to_all | solution.py:349
  103.4 0.0 copy-done.1
  103.4 0.2 copy.11
  103.6 4.5 %token_side.1 = bf16[4,256,1280]{2,1,0:T(8,128)(2,1)} custom-call(f32[4,256,128]{2,1,0:T(8,128)} %fusion.12.disp_hbm.disp_ref, bf16[4,256,128]{2,1,0:T(8,128)(2,1)S(1)} %get-tuple-element.9.lg_ref, bf16[4,128,1280]{2,1,0:T(8,128)(2,1)} %get-tuple-element.10.sb_ref, bf16[128,1280]{1,0:T(8,128)(2,1)S(1)} %bitcast.17), custom_call_target="tpu_custom_call" | custom-call | flops 671088640 | bytes 5242880 | tf_op jit(solution)/shard_map/token_side/pallas_call | solution.py:287
  108.1 7.4 %all-to-all-done.3.x_ref = bf16[128,2,640]{2,1,0:T(2,128)(2,1)S(1)} async-done(((bf16[128,2,640]{2,1,0:T(2,128)(2,1)}), bf16[128,2,640]{2,1,0:T(2,128)(2,1)S(1)}, u32[]{:S(2)}, u32[]{:S(2)}) %all-to-all-start.3) | async-done | bytes 327712 | tf_op jit(solution)/shard_map/all_to_all | solution.py:349
  115.6 1.2 %finish.1 = f32[1280,128]{1,0:T(8,128)} custom-call(bf16[128,2,640]{2,1,0:T(2,128)(2,1)S(1)} %all-to-all-done.3.x_ref), custom_call_target="tpu_custom_call" | custom-call | flops 163840 | bytes 983040 | tf_op jit(solution)/shard_map/finish/pallas_call | solution.py:337
Async XLA Ops:
  0.6 58.9 %copy-start = (bf16[4,128,1280]{2,1,0:T(8,128)(2,1)S(1)}, bf16[4,128,1280]{2,1,0:T(8,128)(2,1)}, u32[]{:S(2)}) copy-start(bf16[4,128,1280]{2,1,0:T(8,128)(2,1)} %param.10) | copy-start | bytes 3932164
  5.7 33.5 %all-to-all-start = ((bf16[128,8,640]{2,1,0:T(8,128)(2,1)}), bf16[128,8,640]{2,1,0:T(8,128)(2,1)S(1)}, u32[]{:S(2)}, u32[]{:S(2)}) async-start(bf16[128,8,640]{2,1,0:T(8,128)(2,1)} %bitcast.20), calls=%async_computation | async-start | bytes 2621440 | tf_op jit(solution)/shard_map/all_to_all | solution.py:349
  51.3 26.4 %all-to-all-start.1 = ((bf16[128,8,640]{2,1,0:T(8,128)(2,1)}), bf16[128,8,640]{2,1,0:T(8,128)(2,1)S(1)}, u32[]{:S(2)}, u32[]{:S(2)}) async-start(bf16[128,8,640]{2,1,0:T(8,128)(2,1)} %bitcast.19), calls=%async_computation.1 | async-start | bytes 2621440 | tf_op jit(solution)/shard_map/all_to_all | solution.py:349
  77.7 25.8 %copy-start.1 = (bf16[1280,128]{1,0:T(8,128)(2,1)S(1)}, bf16[1280,128]{1,0:T(8,128)(2,1)}, u32[]{:S(2)}) copy-start(bf16[1280,128]{1,0:T(8,128)(2,1)} %router_hbm.1) | copy-start | bytes 983044
  99.5 16.0 %all-to-all-start.3 = ((bf16[128,2,640]{2,1,0:T(2,128)(2,1)}), bf16[128,2,640]{2,1,0:T(2,128)(2,1)S(1)}, u32[]{:S(2)}, u32[]{:S(2)}) async-start(bf16[128,2,640]{2,1,0:T(2,128)(2,1)} %sum_terms.1), calls=%async_computation.3 | async-start | bytes 655360 | tf_op jit(solution)/shard_map/all_to_all | solution.py:349

commit v4 on v3

--- a/solution.py
+++ b/solution.py
@@ -113,6 +113,34 @@
     )(hbm(tokens), hbm(router), hbm(cotangent))
 
 
+def routing_kernel(logits_ref, cot_ref, out_ref, disp_ref, fc_ref):
+    logits = logits_ref[0]
+    disp_ref[0] = softmax(logits, 0)
+    combine = softmax(logits, 1)
+    grad = dot(cot_ref[0], out_ref[0], 1, 1)
+    fc_ref[0] = combine * (grad - jnp.sum(combine * grad, axis=1, keepdims=True))
+
+
+def routing(logits, cotangent, slot_out):
+    images, m, experts = logits.shape
+    d = cotangent.shape[2]
+    small = pl.BlockSpec((1, m, experts), lambda b: (b, 0, 0))
+    return pl.pallas_call(
+        routing_kernel,
+        grid=(images,),
+        in_specs=[
+            small,
+            pl.BlockSpec((1, m, d), lambda b: (b, 0, 0)),
+            pl.BlockSpec((1, experts, d), lambda b: (b, 0, 0)),
+        ],
+        out_specs=[small, small],
+        out_shape=[pltpu.HBM(logits.shape, F32)] * 2,
+        compiler_params=pltpu.CompilerParams(vmem_limit_bytes=32 * MIB),
+        cost_estimate=cost(2 * images * m * d * experts, 2 * (cotangent.size + slot_out.size) + 12 * logits.size),
+        name="routing",
+    )(hbm(logits), hbm(cotangent), hbm(slot_out))
+
+
 UP_CUTS = (0, 1024, 2560)
 BACK_CUTS = (0, 1280)
 WINDOW = 2
@@ -122,7 +150,7 @@
     return [(lo * size // cuts[-1], hi * size // cuts[-1]) for lo, hi in zip(cuts, cuts[1:])]
 
 
-def expert_kernel(x_ref, wo_hbm, wi_hbm, slope_hbm, out_hbm, wo, wi, slope, out, wide, rows_ref, pg_ref, w_sems, slope_sems, out_sems):
+def expert_kernel(x_ref, wo_hbm, wi_hbm, slope_hbm, out, wo, wi, slope, wide, rows_ref, pg_ref, w_sems, slope_sems):
     half_tiles, total, _ = wide.shape
     count = total // 2
     ff, d = wo.shape
@@ -159,25 +187,19 @@
         arrive(i)
         hidden = dot(rows_ref[...], wo[lo:hi, :], 1, 1)
         pg_ref[:, lo:hi] = (hidden * slope[:, lo:hi]).astype(BF)
-    done, sent = set(), []
+    done = set()
     for i, (lo, hi) in enumerate(backs):
         arrive(len(ups) + i)
-        back = dot(pg_ref[...], wi[lo:hi, :], 1, 1)
         for t in range(lo // LANES, hi // LANES):
             h, j = divmod(t, half_tiles)
-            at = t * LANES - lo
+            at = j * LANES
+            if j == 0:
+                back = dot(pg_ref[...], wi[t * LANES : t * LANES + d // 2, :], 1, 1)
             wide[j, pl.ds(h, count, 2), :] = back[:, at : at + LANES]
             done.add(t)
             if {j, j + half_tiles} <= done:
                 cols = slice(j * LANES, (j + 1) * LANES)
                 out[:, cols] = wide[j].astype(BF)
-                copy = pltpu.make_async_copy(
-                    out.at[:, pl.ds(j * LANES, LANES)], out_hbm.at[:, pl.ds(j * LANES, LANES)], out_sems.at[j]
-                )
-                copy.start()
-                sent.append(copy)
-    for copy in sent:
-        copy.wait()
 
 
 def expert(x, w_out, w_in, slope):
@@ -187,19 +209,17 @@
     return pl.pallas_call(
         expert_kernel,
         in_specs=[WHOLE, raw, raw, raw],
-        out_specs=raw,
-        out_shape=pltpu.HBM((total, half), BF),
+        out_specs=WHOLE,
+        out_shape=pltpu.VMEM((total, half), BF),
         scratch_shapes=[
             pltpu.VMEM((ff, d), BF),
             pltpu.VMEM((d, ff), BF),
             pltpu.VMEM(slope.shape, slope.dtype),
-            pltpu.VMEM((total, half), BF),
             pltpu.VMEM((half // LANES, total, LANES), F32),
             pltpu.VMEM((total // 2, d), BF),
             pltpu.VMEM((total // 2, ff), BF),
             pltpu.SemaphoreType.DMA((len(UP_CUTS) + len(BACK_CUTS) - 2,)),
             pltpu.SemaphoreType.DMA((len(UP_CUTS) - 1,)),
-            pltpu.SemaphoreType.DMA((half // LANES,)),
         ],
         compiler_params=pltpu.CompilerParams(vmem_limit_bytes=56 * MIB),
         cost_estimate=cost(2 * total * d * ff, 4 * ff * d + 2 * total * ff),
@@ -208,7 +228,7 @@
 
 
 def back_kernel(
-    y_ref, tok_hbm, disp_hbm, fc_hbm, lg_ref, sb_hbm, term_hbm, wide, tok, disp, fc, sb, lg_t, term_ref, in_sems, out_sems
+    y_ref, tok_hbm, disp_hbm, fc_hbm, lg_ref, sb_hbm, term_ref, wide, tok, disp, fc, sb, lg_t, in_sems, out_sems
 ):
     half_tiles, total, _ = wide.shape
     images, experts, d = sb.shape
@@ -226,21 +246,18 @@
             sb[b, :, t * LANES : (t + 1) * LANES] = wide[j, pl.ds(2 * b + h, experts, stride), :].astype(BF)
     for copy in arrivals:
         copy.wait()
+    sb_copy = pltpu.make_async_copy(sb, sb_hbm, out_sems.at[0])
+    sb_copy.start()
     for b in range(images):
         grad = dot(tok[b], sb[b], 1, 1)
         from_dispatch = disp[b] * (grad - jnp.sum(disp[b] * grad, axis=0, keepdims=True))
         logit_grad = fc[b] + from_dispatch
         lg_ref[b] = logit_grad.astype(BF)
         lg_t[:, b * m : (b + 1) * m] = logit_grad.T.astype(BF)
-    sb_copy = pltpu.make_async_copy(sb, sb_hbm, out_sems.at[0])
-    sb_copy.start()
     term = dot(lg_t[...], tok[...].reshape(images * m, d), 1, 0)
     for h in range(2):
         term_ref[:, h, :] = term[:, h * (d // 2) : (h + 1) * (d // 2)].astype(BF)
-    term_copy = pltpu.make_async_copy(term_ref, term_hbm, out_sems.at[1])
-    term_copy.start()
     sb_copy.wait()
-    term_copy.wait()
 
 
 def back(y, tokens, dispatch, from_combine):
@@ -251,11 +268,11 @@
     return pl.pallas_call(
         back_kernel,
         in_specs=[WHOLE, raw, raw, raw],
-        out_specs=[WHOLE, raw, raw],
+        out_specs=[WHOLE, raw, WHOLE],
         out_shape=[
             pltpu.VMEM((images, m, experts), BF),
             pltpu.HBM((images, experts, d), BF),
-            pltpu.HBM((experts, 2, d // 2), BF),
+            pltpu.VMEM((experts, 2, d // 2), BF),
         ],
         scratch_shapes=[
             pltpu.VMEM((half // LANES, total, LANES), F32),
@@ -264,9 +281,8 @@
             pltpu.VMEM((images, m, experts), F32),
             pltpu.VMEM((images, experts, d), BF),
             pltpu.VMEM((experts, images * m), BF),
-            pltpu.VMEM((experts, 2, d // 2), BF),
             pltpu.SemaphoreType.DMA((3,)),
-            pltpu.SemaphoreType.DMA((2,)),
+            pltpu.SemaphoreType.DMA((1,)),
         ],
         compiler_params=pltpu.CompilerParams(vmem_limit_bytes=32 * MIB),
         cost_estimate=cost(4 * images * m * d * experts, 4 * images * m * d),
@@ -322,14 +338,20 @@
     )(vmem(x))
 
 
-def finish_kernel(x_ref, out_ref):
+def finish_kernel(x_ref, out_hbm, out_ref, sems):
     half = x_ref.shape[2]
     wide = x_ref[...].astype(F32)
+    sent = []
     for h in range(2):
         part = wide[:, h, :]
         for t in range(half // LANES):
             row = h * half + t * LANES
             out_ref[row : row + LANES, :] = part[:, t * LANES : (t + 1) * LANES].T
+        rows = pl.ds(h * half, half)
+        sent.append(pltpu.make_async_copy(out_ref.at[rows], out_hbm.at[rows], sems.at[h]))
+        sent[-1].start()
+    for copy in sent:
+        copy.wait()
 
 
 def finish(x):
@@ -337,8 +359,9 @@
     return pl.pallas_call(
         finish_kernel,
         in_specs=[WHOLE],
-        out_specs=WHOLE,
+        out_specs=pl.BlockSpec(memory_space=pl.ANY),
         out_shape=pltpu.HBM((two * half, experts), F32),
+        scratch_shapes=[pltpu.VMEM((two * half, experts), F32), pltpu.SemaphoreType.DMA((2,))],
         compiler_params=pltpu.CompilerParams(vmem_limit_bytes=24 * MIB),
         cost_estimate=cost(x.size, 6 * x.size),
         name="finish",
@@ -361,10 +384,8 @@
     arrived = exchange_rows(slot_grad, devices)
 
     slope = gelu_slope(pre_act[0].astype(F32))
-    combine = jax.nn.softmax(logits, axis=2)
-    dispatch = jax.nn.softmax(logits, axis=1)
-    combine_grad = jnp.einsum("bmd,bed->bme", cotangent, slot_out, preferred_element_type=F32)
-    from_combine = combine * (combine_grad - jnp.sum(combine * combine_grad, axis=2, keepdims=True))
+    dispatch, from_combine = routing(logits, cotangent, slot_out)
+    slope, dispatch, from_combine = lax.optimization_barrier((slope, dispatch, from_combine))
 
     slot_back = expert(arrived, w_out[0], w_in[0], slope)
     returned = exchange_rows(slot_back, devices)

time: 117 us -> 114 us (0.974)
  blocking collectives: 16.7 us -> 41.7 us
  waiting for transfers between devices: 37.1 us -> 20.8 us
  other arithmetic: 9.51 us -> 3.8 us
  matrix products: 4.84 us -> 0 us
  starting transfers between devices: 19.6 us -> 15.4 us
  Pallas kernels: 28.1 us -> 30.9 us
    all_to_all x1 -> x2, blocking collectives: 16.7 us -> 41.7 us  [exchange(): return lax.all_to_all(x, AXES, split_axis=0, concat_axis=0, tiled=True)]
    all_to_all x3 -> x2, waiting for transfers between devices: 37.1 us -> 20.8 us  [exchange(): return lax.all_to_all(x, AXES, split_axis=0, concat_axis=0, tiled=True)]
    sub x1 -> x0, matrix products: 4.84 us -> none  [local(): combine_grad - jnp.sum(combine * combine_grad, axis=2, keepdims=True)]
    pallas_call x1 -> x2, Pallas kernels: 1.21 us -> 5.97 us  [the longest x1 4.82 us: routing(): pl.pallas_call(routing_kernel, grid=(images,), in_specs=[small, pl.BlockS...]
    all_to_all x3 -> x2, starting transfers between devices: 19.6 us -> 15.4 us  [exchange(): return lax.all_to_all(x, AXES, split_axis=0, concat_axis=0, tiled=True)]
    div x2 -> x0, other arithmetic: 3.93 us -> none  [the longest x1 2.29 us: local(): dispatch = jax.nn.softmax(logits, axis=1)]
    add x1, other arithmetic: 5.58 us -> 3.8 us  [gelu_slope(): return normal_cdf + values * density]
  transfers between devices with their start and end apart: 3 -> 2, of which waited for: 3 -> 2; matrix products, arithmetic and copies ran while one was open for 12% -> 4% of each run, Pallas kernels for 4% -> 8%
where the time goes in v4:
time: 114 us
  blocking collectives  41.7 us (37%)
  Pallas kernels  30.9 us (27%)
  waiting for transfers between devices  20.8 us (18%)
  starting transfers between devices  15.4 us (14%)
  other arithmetic  3.8 us (3%)
    all_to_all x2, blocking collectives, exchange(): return lax.all_to_all(x, AXES, split_axis=0, concat_axis=0, tiled=True)  41.7 us
    all_to_all x2, waiting for transfers between devices, exchange(): return lax.all_to_all(x, AXES, split_axis=0, concat_axis=0, tiled=True)  20.8 us
    all_to_all x2, starting transfers between devices, exchange(): return lax.all_to_all(x, AXES, split_axis=0, concat_axis=0, tiled=True)  15.4 us
    pallas_call x1, Pallas kernels, expert(): pl.pallas_call(expert_kernel, in_specs=[WHOLE, raw, raw, raw], out_specs=...  11.1 us
    pallas_call x1, Pallas kernels, front(): pl.pallas_call(front_kernel, in_specs=[raw] * 3, out_specs=[raw] * 2, out...  4.93 us
    pallas_call x1, Pallas kernels, routing(): pl.pallas_call(routing_kernel, grid=(images,), in_specs=[small, pl.BlockS...  4.82 us
    pallas_call x1, Pallas kernels, token_side(): pl.pallas_call(token_kernel, grid=(images,), in_specs=[pl.BlockSpec((1, m...  4.49 us
    add x1, other arithmetic, gelu_slope(): return normal_cdf + values * density  3.8 us
  transfers between devices with their start and end apart: 2, of which 2 were waited for; matrix products, arithmetic and copies ran while one was open for 4% of the time, Pallas kernels for 8%

profile of v4, /device:TPU:1, one launch (start us, length us, event | category | flops | bytes accessed | tf_op | source)
XLA Modules:
  0.0 113.6 jit_solution(1635086843823505796)
XLA Ops:
  0.6 4.9 %front.1 = (bf16[1024,640]{1,0:T(8,128)(2,1)}, f32[4,256,128]{2,1,0:T(8,128)}) custom-call(bf16[4,256,1280]{2,1,0:T(8,128)(2,1)} %tok_hbm.3, bf16[1280,128]{1,0:T(8,128)(2,1)} %router_hbm.1, bf16[4,256,1280]{2,1,0:T(8,128)(2,1)} %cot_ref.1), custom_call_target="tpu_custom_call" | custom-call | flops 671088640 | bytes 10485760 | tf_op jit(solution)/shard_map/front/pallas_call | solution.py:90
  5.6 11.5 %all-to-all-start = ((bf16[128,8,640]{2,1,0:T(8,128)(2,1)}), bf16[128,8,640]{2,1,0:T(8,128)(2,1)S(1)}, u32[]{:S(2)}, u32[]{:S(2)}) async-start(bf16[128,8,640]{2,1,0:T(8,128)(2,1)} %bitcast.14), calls=%async_computation | async-start | bytes 2621440 | tf_op jit(solution)/shard_map/all_to_all | solution.py:372
  17.1 0.0 copy-start
  17.1 4.8 %routing.1 = (f32[4,256,128]{2,1,0:T(8,128)}, f32[4,256,128]{2,1,0:T(8,128)}) custom-call(f32[4,256,128]{2,1,0:T(8,128)} %get-tuple-element.12.logits_ref, bf16[4,256,1280]{2,1,0:T(8,128)(2,1)} %cot_ref.1, bf16[4,128,1280]{2,1,0:T(8,128)(2,1)} %out_ref.1), custom_call_target="tpu_custom_call" | custom-call | flops 335544320 | bytes 5505024 | tf_op jit(solution)/shard_map/routing/pallas_call | solution.py:128
  21.9 0.0 copy-done
  21.9 3.8 %fusion.3.slope_hbm = f32[512,2560]{1,0:T(8,128)} fusion(bf16[1,512,2560]{2,1,0:T(8,128)(2,1)S(1)} %copy-done), kind=kLoop, calls=%fused_computation.7 | loop fusion | flops 11796480 | bytes 7864320 | tf_op jit(solution)/shard_map/add | solution.py:36
  25.7 13.3 %all-to-all-done = bf16[128,8,640]{2,1,0:T(8,128)(2,1)S(1)} async-done(((bf16[128,8,640]{2,1,0:T(8,128)(2,1)}), bf16[128,8,640]{2,1,0:T(8,128)(2,1)S(1)}, u32[]{:S(2)}, u32[]{:S(2)}) %all-to-all-start) | async-done | bytes 1310752 | tf_op jit(solution)/shard_map/all_to_all | solution.py:372
  39.0 11.1 %expert.1 = bf16[1024,640]{1,0:T(8,128)(2,1)S(1)} custom-call(bf16[1024,640]{1,0:T(8,128)(2,1)S(1)} %bitcast.12, bf16[2560,1280]{1,0:T(8,128)(2,1)} %bitcast.15, bf16[1280,2560]{1,0:T(8,128)(2,1)} %bitcast.16, f32[512,2560]{1,0:T(8,128)} %fusion.3.slope_hbm), custom_call_target="tpu_custom_call" | custom-call | flops 6710886400 | bytes 18350080 | tf_op jit(solution)/shard_map/expert/pallas_call | solution.py:209
  50.2 0.0 copy-start.1
  50.2 25.8 %all_to_all.20 = bf16[128,8,640]{2,1,0:T(8,128)(2,1)S(1)} all-to-all(bf16[128,8,640]{2,1,0:T(8,128)(2,1)S(1)} %bitcast.13), channel_id=1, replica_groups=mesh['dp'=8,'expert'=16] {'dp','expert'}, dimensions={0} | all-to-all | bytes 2621440 | tf_op jit(solution)/shard_map/all_to_all | solution.py:372
  76.0 3.6 %back.1 = (bf16[4,256,128]{2,1,0:T(8,128)(2,1)S(1)}, bf16[4,128,1280]{2,1,0:T(8,128)(2,1)}, bf16[128,2,640]{2,1,0:T(2,128)(2,1)S(1)}) custom-call(bf16[1024,640]{1,0:T(8,128)(2,1)S(1)} %bitcast.10, bf16[4,256,1280]{2,1,0:T(8,128)(2,1)} %tok_hbm.3, f32[4,256,128]{2,1,0:T(8,128)} %get-tuple-element.15.disp_hbm.disp_ref, f32[4,256,128]{2,1,0:T(8,128)} %get-tuple-element.18.fc_hbm), custom_call_target="tpu_custom_call" | custom-call | flops 671088640 | bytes 5242880 | tf_op jit(solution)/shard_map/back/pallas_call | solution.py:268
  79.6 15.9 %all_to_all.21.x_ref = bf16[128,2,640]{2,1,0:T(2,128)(2,1)S(1)} all-to-all(bf16[128,2,640]{2,1,0:T(2,128)(2,1)S(1)} %get-tuple-element.21), channel_id=1, replica_groups=mesh['dp'=8,'expert'=16] {'dp','expert'}, dimensions={0} | all-to-all | bytes 655360 | tf_op jit(solution)/shard_map/all_to_all | solution.py:372
  95.4 0.8 sum_terms.1
  96.3 3.9 %all-to-all-start.3 = ((bf16[128,2,640]{2,1,0:T(2,128)(2,1)}), bf16[128,2,640]{2,1,0:T(2,128)(2,1)S(1)}, u32[]{:S(2)}, u32[]{:S(2)}) async-start(bf16[128,2,640]{2,1,0:T(2,128)(2,1)} %sum_terms.1), calls=%async_computation.3 | async-start | bytes 655360 | tf_op jit(solution)/shard_map/all_to_all | solution.py:372
  100.2 0.0 copy-done.1
  100.2 0.2 copy.9
  100.4 4.5 %token_side.1 = bf16[4,256,1280]{2,1,0:T(8,128)(2,1)} custom-call(f32[4,256,128]{2,1,0:T(8,128)} %get-tuple-element.15.disp_hbm.disp_ref, bf16[4,256,128]{2,1,0:T(8,128)(2,1)S(1)} %get-tuple-element.19.lg_ref, bf16[4,128,1280]{2,1,0:T(8,128)(2,1)} %get-tuple-element.20.sb_ref, bf16[128,1280]{1,0:T(8,128)(2,1)S(1)} %bitcast.11), custom_call_target="tpu_custom_call" | custom-call | flops 671088640 | bytes 5242880 | tf_op jit(solution)/shard_map/token_side/pallas_call | solution.py:303
  104.9 7.4 %all-to-all-done.3.x_ref = bf16[128,2,640]{2,1,0:T(2,128)(2,1)S(1)} async-done(((bf16[128,2,640]{2,1,0:T(2,128)(2,1)}), bf16[128,2,640]{2,1,0:T(2,128)(2,1)S(1)}, u32[]{:S(2)}, u32[]{:S(2)}) %all-to-all-start.3) | async-done | bytes 327712 | tf_op jit(solution)/shard_map/all_to_all | solution.py:372
  112.3 1.2 %finish.1 = f32[1280,128]{1,0:T(8,128)} custom-call(bf16[128,2,640]{2,1,0:T(2,128)(2,1)S(1)} %all-to-all-done.3.x_ref), custom_call_target="tpu_custom_call" | custom-call | flops 163840 | bytes 983040 | tf_op jit(solution)/shard_map/finish/pallas_call | solution.py:359
Async XLA Ops:
  5.6 33.5 %all-to-all-start = ((bf16[128,8,640]{2,1,0:T(8,128)(2,1)}), bf16[128,8,640]{2,1,0:T(8,128)(2,1)S(1)}, u32[]{:S(2)}, u32[]{:S(2)}) async-start(bf16[128,8,640]{2,1,0:T(8,128)(2,1)} %bitcast.14), calls=%async_computation | async-start | bytes 2621440 | tf_op jit(solution)/shard_map/all_to_all | solution.py:372
  17.1 4.8 %copy-start = (bf16[1,512,2560]{2,1,0:T(8,128)(2,1)S(1)}, bf16[1,512,2560]{2,1,0:T(8,128)(2,1)}, u32[]{:S(2)}) copy-start(bf16[1,512,2560]{2,1,0:T(8,128)(2,1)} %param.11) | copy-start | bytes 7864324
  50.2 50.0 %copy-start.1 = (bf16[1280,128]{1,0:T(8,128)(2,1)S(1)}, bf16[1280,128]{1,0:T(8,128)(2,1)}, u32[]{:S(2)}) copy-start(bf16[1280,128]{1,0:T(8,128)(2,1)} %router_hbm.1) | copy-start | bytes 983044
  96.3 16.0 %all-to-all-start.3 = ((bf16[128,2,640]{2,1,0:T(2,128)(2,1)}), bf16[128,2,640]{2,1,0:T(2,128)(2,1)S(1)}, u32[]{:S(2)}, u32[]{:S(2)}) async-start(bf16[128,2,640]{2,1,0:T(2,128)(2,1)} %sum_terms.1), calls=%async_computation.3 | async-start | bytes 655360 | tf_op jit(solution)/shard_map/all_to_all | solution.py:372

commit v5 on v4

--- a/solution.py
+++ b/solution.py
@@ -141,7 +141,7 @@
     )(hbm(logits), hbm(cotangent), hbm(slot_out))
 
 
-UP_CUTS = (0, 1024, 2560)
+UP_CUTS = (0, 640, 1536, 2560)
 BACK_CUTS = (0, 1280)
 WINDOW = 2
 
@@ -176,13 +176,14 @@
         if i + WINDOW < len(groups):
             start(i + WINDOW)
 
-    for i in range(WINDOW):
-        start(i)
+    start(0)
     for j in range(half_tiles):
         wide[j] = x_ref[:, j * LANES : (j + 1) * LANES].astype(F32)
     for t in range(2 * half_tiles):
         h, j = divmod(t, half_tiles)
         rows_ref[:, t * LANES : (t + 1) * LANES] = wide[j, pl.ds(h, count, 2), :].astype(BF)
+    for i in range(1, WINDOW):
+        start(i)
     for i, (lo, hi) in enumerate(ups):
         arrive(i)
         hidden = dot(rows_ref[...], wo[lo:hi, :], 1, 1)
@@ -235,6 +236,8 @@
     m = tok.shape[1]
     stride = total // experts
     pairs = ((tok_hbm, tok), (disp_hbm, disp), (fc_hbm, fc))
+    cut = images // 2
+    pairs = [(src.at[p], dst.at[p]) for p in (pl.ds(0, cut), pl.ds(cut, images - cut)) for src, dst in pairs]
     arrivals = [pltpu.make_async_copy(src, dst, in_sems.at[i]) for i, (src, dst) in enumerate(pairs)]
     for copy in arrivals:
         copy.start()
@@ -244,11 +247,14 @@
         for t in range(2 * half_tiles):
             h, j = divmod(t, half_tiles)
             sb[b, :, t * LANES : (t + 1) * LANES] = wide[j, pl.ds(2 * b + h, experts, stride), :].astype(BF)
-    for copy in arrivals:
+    for copy in arrivals[:3]:
         copy.wait()
     sb_copy = pltpu.make_async_copy(sb, sb_hbm, out_sems.at[0])
     sb_copy.start()
     for b in range(images):
+        if b == cut:
+            for copy in arrivals[3:]:
+                copy.wait()
         grad = dot(tok[b], sb[b], 1, 1)
         from_dispatch = disp[b] * (grad - jnp.sum(disp[b] * grad, axis=0, keepdims=True))
         logit_grad = fc[b] + from_dispatch
@@ -281,7 +287,7 @@
             pltpu.VMEM((images, m, experts), F32),
             pltpu.VMEM((images, experts, d), BF),
             pltpu.VMEM((experts, images * m), BF),
-            pltpu.SemaphoreType.DMA((3,)),
+            pltpu.SemaphoreType.DMA((6,)),
             pltpu.SemaphoreType.DMA((1,)),
         ],
         compiler_params=pltpu.CompilerParams(vmem_limit_bytes=32 * MIB),

time: 114 us -> 113 us (level)
  no operation moved by 1% of the time
where the time goes in v5:
time: 113 us
  blocking collectives  41.7 us (37%)
  Pallas kernels  30.6 us (27%)
  waiting for transfers between devices  20.8 us (18%)
  starting transfers between devices  15.4 us (14%)
  other arithmetic  3.8 us (3%)
    all_to_all x2, blocking collectives, exchange(): return lax.all_to_all(x, AXES, split_axis=0, concat_axis=0, tiled=True)  41.7 us
    all_to_all x2, waiting for transfers between devices, exchange(): return lax.all_to_all(x, AXES, split_axis=0, concat_axis=0, tiled=True)  20.8 us
    all_to_all x2, starting transfers between devices, exchange(): return lax.all_to_all(x, AXES, split_axis=0, concat_axis=0, tiled=True)  15.4 us
    pallas_call x1, Pallas kernels, expert(): pl.pallas_call(expert_kernel, in_specs=[WHOLE, raw, raw, raw], out_specs=...  11 us
    pallas_call x1, Pallas kernels, front(): pl.pallas_call(front_kernel, in_specs=[raw] * 3, out_specs=[raw] * 2, out...  4.93 us
    pallas_call x1, Pallas kernels, routing(): pl.pallas_call(routing_kernel, grid=(images,), in_specs=[small, pl.BlockS...  4.82 us
    pallas_call x1, Pallas kernels, token_side(): pl.pallas_call(token_kernel, grid=(images,), in_specs=[pl.BlockSpec((1, m...  4.49 us
    add x1, other arithmetic, gelu_slope(): return normal_cdf + values * density  3.8 us
  transfers between devices with their start and end apart: 2, of which 2 were waited for; matrix products, arithmetic and copies ran while one was open for 4% of the time, Pallas kernels for 8%

profile of v5, /device:TPU:1, one launch (start us, length us, event | category | flops | bytes accessed | tf_op | source)
XLA Modules:
  0.0 113.1 jit_solution(16174376454731884173)
XLA Ops:
  0.6 4.9 %front.1 = (bf16[1024,640]{1,0:T(8,128)(2,1)}, f32[4,256,128]{2,1,0:T(8,128)}) custom-call(bf16[4,256,1280]{2,1,0:T(8,128)(2,1)} %tok_hbm.3, bf16[1280,128]{1,0:T(8,128)(2,1)} %router_hbm.1, bf16[4,256,1280]{2,1,0:T(8,128)(2,1)} %cot_ref.1), custom_call_target="tpu_custom_call" | custom-call | flops 671088640 | bytes 10485760 | tf_op jit(solution)/shard_map/front/pallas_call | solution.py:90
  5.6 11.5 %all-to-all-start = ((bf16[128,8,640]{2,1,0:T(8,128)(2,1)}), bf16[128,8,640]{2,1,0:T(8,128)(2,1)S(1)}, u32[]{:S(2)}, u32[]{:S(2)}) async-start(bf16[128,8,640]{2,1,0:T(8,128)(2,1)} %bitcast.14), calls=%async_computation | async-start | bytes 2621440 | tf_op jit(solution)/shard_map/all_to_all | solution.py:378
  17.1 0.0 copy-start
  17.1 4.8 %routing.1 = (f32[4,256,128]{2,1,0:T(8,128)}, f32[4,256,128]{2,1,0:T(8,128)}) custom-call(f32[4,256,128]{2,1,0:T(8,128)} %get-tuple-element.12.logits_ref, bf16[4,256,1280]{2,1,0:T(8,128)(2,1)} %cot_ref.1, bf16[4,128,1280]{2,1,0:T(8,128)(2,1)} %out_ref.1), custom_call_target="tpu_custom_call" | custom-call | flops 335544320 | bytes 5505024 | tf_op jit(solution)/shard_map/routing/pallas_call | solution.py:128
  21.9 0.0 copy-done
  21.9 3.8 %fusion.3.slope_hbm = f32[512,2560]{1,0:T(8,128)} fusion(bf16[1,512,2560]{2,1,0:T(8,128)(2,1)S(1)} %copy-done), kind=kLoop, calls=%fused_computation.7 | loop fusion | flops 11796480 | bytes 7864320 | tf_op jit(solution)/shard_map/add | solution.py:36
  25.7 13.3 %all-to-all-done = bf16[128,8,640]{2,1,0:T(8,128)(2,1)S(1)} async-done(((bf16[128,8,640]{2,1,0:T(8,128)(2,1)}), bf16[128,8,640]{2,1,0:T(8,128)(2,1)S(1)}, u32[]{:S(2)}, u32[]{:S(2)}) %all-to-all-start) | async-done | bytes 1310752 | tf_op jit(solution)/shard_map/all_to_all | solution.py:378
  39.0 11.0 %expert.1 = bf16[1024,640]{1,0:T(8,128)(2,1)S(1)} custom-call(bf16[1024,640]{1,0:T(8,128)(2,1)S(1)} %bitcast.12, bf16[2560,1280]{1,0:T(8,128)(2,1)} %bitcast.15, bf16[1280,2560]{1,0:T(8,128)(2,1)} %bitcast.16, f32[512,2560]{1,0:T(8,128)} %fusion.3.slope_hbm), custom_call_target="tpu_custom_call" | custom-call | flops 6710886400 | bytes 18350080 | tf_op jit(solution)/shard_map/expert/pallas_call | solution.py:210
  50.0 0.0 copy-start.1
  50.0 25.8 %all_to_all.20 = bf16[128,8,640]{2,1,0:T(8,128)(2,1)S(1)} all-to-all(bf16[128,8,640]{2,1,0:T(8,128)(2,1)S(1)} %bitcast.13), channel_id=1, replica_groups=mesh['dp'=8,'expert'=16] {'dp','expert'}, dimensions={0} | all-to-all | bytes 2621440 | tf_op jit(solution)/shard_map/all_to_all | solution.py:378
  75.8 3.4 %back.1 = (bf16[4,256,128]{2,1,0:T(8,128)(2,1)S(1)}, bf16[4,128,1280]{2,1,0:T(8,128)(2,1)}, bf16[128,2,640]{2,1,0:T(2,128)(2,1)S(1)}) custom-call(bf16[1024,640]{1,0:T(8,128)(2,1)S(1)} %bitcast.10, bf16[4,256,1280]{2,1,0:T(8,128)(2,1)} %tok_hbm.3, f32[4,256,128]{2,1,0:T(8,128)} %get-tuple-element.15.disp_hbm.disp_ref, f32[4,256,128]{2,1,0:T(8,128)} %get-tuple-element.18.fc_hbm), custom_call_target="tpu_custom_call" | custom-call | flops 671088640 | bytes 5242880 | tf_op jit(solution)/shard_map/back/pallas_call | solution.py:274
  79.2 15.9 %all_to_all.21.x_ref = bf16[128,2,640]{2,1,0:T(2,128)(2,1)S(1)} all-to-all(bf16[128,2,640]{2,1,0:T(2,128)(2,1)S(1)} %get-tuple-element.21), channel_id=1, replica_groups=mesh['dp'=8,'expert'=16] {'dp','expert'}, dimensions={0} | all-to-all | bytes 655360 | tf_op jit(solution)/shard_map/all_to_all | solution.py:378
  95.1 0.8 sum_terms.1
  95.9 3.9 %all-to-all-start.3 = ((bf16[128,2,640]{2,1,0:T(2,128)(2,1)}), bf16[128,2,640]{2,1,0:T(2,128)(2,1)S(1)}, u32[]{:S(2)}, u32[]{:S(2)}) async-start(bf16[128,2,640]{2,1,0:T(2,128)(2,1)} %sum_terms.1), calls=%async_computation.3 | async-start | bytes 655360 | tf_op jit(solution)/shard_map/all_to_all | solution.py:378
  99.8 0.0 copy-done.1
  99.8 0.2 copy.9
  100.0 4.5 %token_side.1 = bf16[4,256,1280]{2,1,0:T(8,128)(2,1)} custom-call(f32[4,256,128]{2,1,0:T(8,128)} %get-tuple-element.15.disp_hbm.disp_ref, bf16[4,256,128]{2,1,0:T(8,128)(2,1)S(1)} %get-tuple-element.19.lg_ref, bf16[4,128,1280]{2,1,0:T(8,128)(2,1)} %get-tuple-element.20.sb_ref, bf16[128,1280]{1,0:T(8,128)(2,1)S(1)} %bitcast.11), custom_call_target="tpu_custom_call" | custom-call | flops 671088640 | bytes 5242880 | tf_op jit(solution)/shard_map/token_side/pallas_call | solution.py:309
  104.5 7.4 %all-to-all-done.3.x_ref = bf16[128,2,640]{2,1,0:T(2,128)(2,1)S(1)} async-done(((bf16[128,2,640]{2,1,0:T(2,128)(2,1)}), bf16[128,2,640]{2,1,0:T(2,128)(2,1)S(1)}, u32[]{:S(2)}, u32[]{:S(2)}) %all-to-all-start.3) | async-done | bytes 327712 | tf_op jit(solution)/shard_map/all_to_all | solution.py:378
  112.0 1.2 %finish.1 = f32[1280,128]{1,0:T(8,128)} custom-call(bf16[128,2,640]{2,1,0:T(2,128)(2,1)S(1)} %all-to-all-done.3.x_ref), custom_call_target="tpu_custom_call" | custom-call | flops 163840 | bytes 983040 | tf_op jit(solution)/shard_map/finish/pallas_call | solution.py:365
Async XLA Ops:
  5.6 33.5 %all-to-all-start = ((bf16[128,8,640]{2,1,0:T(8,128)(2,1)}), bf16[128,8,640]{2,1,0:T(8,128)(2,1)S(1)}, u32[]{:S(2)}, u32[]{:S(2)}) async-start(bf16[128,8,640]{2,1,0:T(8,128)(2,1)} %bitcast.14), calls=%async_computation | async-start | bytes 2621440 | tf_op jit(solution)/shard_map/all_to_all | solution.py:378
  17.1 4.8 %copy-start = (bf16[1,512,2560]{2,1,0:T(8,128)(2,1)S(1)}, bf16[1,512,2560]{2,1,0:T(8,128)(2,1)}, u32[]{:S(2)}) copy-start(bf16[1,512,2560]{2,1,0:T(8,128)(2,1)} %param.11) | copy-start | bytes 7864324
  50.0 49.8 %copy-start.1 = (bf16[1280,128]{1,0:T(8,128)(2,1)S(1)}, bf16[1280,128]{1,0:T(8,128)(2,1)}, u32[]{:S(2)}) copy-start(bf16[1280,128]{1,0:T(8,128)(2,1)} %router_hbm.1) | copy-start | bytes 983044
  95.9 16.0 %all-to-all-start.3 = ((bf16[128,2,640]{2,1,0:T(2,128)(2,1)}), bf16[128,2,640]{2,1,0:T(2,128)(2,1)S(1)}, u32[]{:S(2)}, u32[]{:S(2)}) async-start(bf16[128,2,640]{2,1,0:T(2,128)(2,1)} %sum_terms.1), calls=%async_computation.3 | async-start | bytes 655360 | tf_op jit(solution)/shard_map/all_to_all | solution.py:378
